TPU v7x, 256 devices: a whole 4x4x8 slice. The times are simulated.
256 devices in a mesh: row: 16 (over z_lo, y, core), col: 16 (over x, z_hi).
Axes of the slice: x: 4, y: 4, z: 8 (z_hi: 4, z_lo: 2; z = z_hi * 2 + z_lo), core: 2. Of those that a mesh axis runs over, the one named last changes fastest.
Arguments:
- features: bfloat16 [65536, 128], P(('col', 'row')), may hold values from -6 to 6
- weight: bfloat16 [128, 256], replicated, may hold values from -0.5 to 0.5
- bias: float32 [256], replicated, may hold values from -3 to 3
- cotangent: bfloat16 [65536, 256], P(('row', 'col')), may hold values from -6 to 6
- tile_rows: int32 [16, 16, 160], P('row', 'col'), may hold values from 0 to 31
- tile_cols: int32 [16, 16, 160], P('row', 'col'), may hold values from 0 to 31
- tile_mask: int32 [16, 16, 160, 128, 128], P('row', 'col'), may hold values from 0 to 1, as said below
Outputs:
- activations: bfloat16 [65536, 256], P(('row', 'col'))
- grad_features: bfloat16 [65536, 128], P(('col', 'row'))
- grad_weight: float32 [128, 256], replicated
- grad_bias: float32 [256], replicated
Inputs may be any that keep to these rules, and one draw needn't show every extreme that they name: `tile_mask`: entries are 0 or 1. On each device the slots that hold any entry come first; every such slot has its entry at a = b = 0 set; in every grid row one device has all 160 slots holding entries.
All inputs are finite; a program needn't handle non-finite values.
Results may differ from a plain program's by a relative error of at most 0.0049.
Values may be sent and summed in bfloat16 or wider, within the bound.
A program may use at most 128 MiB of HBM per device.

v0:
```python
import jax
import jax.numpy as jnp
from jax import lax
from jax.sharding import PartitionSpec as P


def select_rows(tile_ids, count):
    return (tile_ids[:, None] == jnp.arange(count, dtype=jnp.int32)[None, :]).astype(jnp.float32)


def on_device(features, weight, bias, cotangent, tile_rows, tile_cols, tile_mask):
    grid_rows = lax.axis_size("row")
    grid_cols = lax.axis_size("col")
    row_pos = lax.axis_index("row")
    col_pos = lax.axis_index("col")
    slot_count = tile_mask.shape[2]
    local_rows = features.shape[0]
    hidden = weight.shape[1]
    row_span = local_rows * grid_cols
    col_span = local_rows * grid_rows
    row_tiles = row_span // 128
    col_tiles = col_span // 128
    entries = tile_mask.reshape(slot_count, 128, 128)
    row_ids = tile_rows.reshape(slot_count)
    col_ids = tile_cols.reshape(slot_count)
    onehot_rows = select_rows(row_ids, row_tiles)
    onehot_cols = select_rows(col_ids, col_tiles)
    row_local = jnp.sum(entries, axis=2).astype(jnp.float32)
    col_local = jnp.sum(entries, axis=1).astype(jnp.float32)
    row_part = jnp.einsum(
        "st,sa->ta", onehot_rows, row_local, precision=lax.Precision.HIGHEST
    ).reshape(row_span)
    col_part = jnp.einsum(
        "st,sb->tb", onehot_cols, col_local, precision=lax.Precision.HIGHEST
    ).reshape(col_span)
    row_count = lax.psum(row_part, "col")
    col_count = lax.psum(col_part, "row")
    row_scale = 1.0 / jnp.sqrt(1.0 + row_count)
    col_scale = 1.0 / jnp.sqrt(1.0 + col_count)
    own_cols = lax.dynamic_slice_in_dim(col_scale, row_pos * local_rows, local_rows, 0)
    own_rows = lax.dynamic_slice_in_dim(row_scale, col_pos * local_rows, local_rows, 0)
    weight_wide = weight.astype(jnp.float32)
    entry_wide = entries.astype(jnp.float32)
    whole_features = lax.all_gather(features, "row", axis=0, tiled=True)
    scaled = (
        jnp.dot(whole_features, weight, preferred_element_type=jnp.float32) * col_scale[:, None]
    )
    width = scaled.shape[1]
    picked = scaled.reshape(col_tiles, 128, width)[col_ids]
    products = jnp.einsum("sab,sbh->sah", entry_wide, picked, precision=lax.Precision.HIGHEST)
    summed = lax.psum_scatter(
        jnp.einsum("st,sah->tah", onehot_rows, products, precision=lax.Precision.HIGHEST).reshape(
            row_span, width
        ),
        "col",
        scatter_dimension=0,
        tiled=True,
    )
    pre_act = own_rows[:, None] * summed + bias[None, :]
    sigmoid_z = jax.nn.sigmoid(pre_act)
    activations = (pre_act * sigmoid_z).astype(jnp.bfloat16)
    grad_pre = cotangent.astype(jnp.float32) * sigmoid_z * (1.0 + pre_act * (1.0 - sigmoid_z))
    sent = (own_rows[:, None] * grad_pre).astype(jnp.bfloat16)
    tile_values = entries.astype(jnp.bfloat16)
    gathered = lax.all_gather(sent, "col", axis=0, tiled=True)
    picked_back = gathered.reshape(row_tiles, 128, hidden)[row_ids]
    back_products = jnp.einsum(
        "sab,sah->sbh", tile_values, picked_back, preferred_element_type=jnp.float32
    )
    spread = jnp.einsum(
        "st,sbh->tbh", onehot_cols, back_products, precision=lax.Precision.HIGHEST
    ).reshape(col_span, hidden)
    column_part = lax.psum_scatter(spread, "row", scatter_dimension=0, tiled=True)
    column_grad = own_cols[:, None] * column_part
    grad_features = jnp.dot(column_grad, weight_wide.T, precision=lax.Precision.HIGHEST).astype(
        jnp.bfloat16
    )
    weight_term = jnp.dot(
        features.astype(jnp.float32).T, column_grad, precision=lax.Precision.HIGHEST
    )
    bias_term = jnp.sum(grad_pre, axis=0)
    weight_total, bias_total = lax.psum((weight_term, bias_term), ("row", "col"))
    factor = 1.0 / jnp.sqrt(jnp.float32(local_rows * grid_rows * grid_cols))
    return (activations, grad_features, weight_total * factor, bias_total * factor)


def solution(mesh):
    placed = (
        P(("col", "row"), None),
        P(),
        P(),
        P(("row", "col"), None),
        P("row", "col", None),
        P("row", "col", None),
        P("row", "col", None, None, None),
    )
    return jax.shard_map(
        on_device,
        mesh=mesh,
        in_specs=placed,
        out_specs=(P(("row", "col"), None), P(("col", "row"), None), P(), P()),
        check_vma=False,
    )
```

profile of v0, /device:TPU:1, one launch (start us, length us, event | category | flops | bytes accessed | tf_op | source)
XLA Modules:
  0.0 711.1 jit_solution(10073522534571437406)
XLA Ops:
  7.2 0.0 copy-start
  7.2 0.0 copy-start.4
  7.2 0.0 all-gather.3.cloned.1.call-start
  7.2 0.7 all-gather.3.cloned.1.call-update
  7.9 0.0 reduce-scatter.3.cloned.1.call-start
  8.0 6.8 fusion.25
  14.7 0.0 copy-done.4
  14.7 0.2 convolution_bitcast_fusion.1
  14.9 53.7 %psum.29 = f32[4096]{0:T(1024)S(1)} all-reduce(f32[4096]{0:T(1024)S(1)} %convolution_bitcast_fusion.1), channel_id=1, replica_groups=mesh['row'=16,'col'=16] {'row'}, use_global_device_ids=true, to_apply=%region_3.0 | all-reduce | flops 4096 | bytes 32768 | tf_op jit(solution)/shard_map/psum | solution.py:37
  68.6 0.0 all-gather.3.cloned.1.call-done
  68.6 0.0 copy-done
  68.6 3.9 convolution_multiply_fusion
  72.5 13.3 %gather_fusion = f32[160,128,256]{2,1,0:T(8,128)} fusion(f32[32,128,256]{2,1,0:T(8,128)} %bitcast.42, s32[1024]{0:T(1024)S(1)} %pad_clamp_fusion.1), kind=kCustom, calls=%fused_computation | custom fusion | bytes 41943680 | tf_op jit(solution)/shard_map/gather | solution.py:49
  85.8 41.7 %fusion.4 = f32[160,256,128]{2,1,0:T(8,128)} fusion(f32[160,128,256]{2,1,0:T(8,128)} %gather_fusion, s32[1,1,160,128,128]{4,3,2,1,0:T(8,128)} %param.13), kind=kOutput, calls=%fused_computation.6 | convolution fusion | flops 8055685120 | bytes 52428800 | tf_op jit(solution)/shard_map/sab,sbh->sah/dot_general | solution.py:50
  127.5 21.3 %copy.15 = f32[160,256,128]{1,0,2:T(8,128)} copy(f32[160,256,128]{2,1,0:T(8,128)} %fusion.4) | data formatting | bytes 41943040 | tf_op jit(solution)/shard_map/sab,sbh->sah/dot_general | solution.py:50
  148.8 0.0 copy-done.3
  148.8 11.7 %fusion.2 = f32[32,128,256]{2,0,1:T(8,128)S(1)} fusion(f32[160,256,128]{1,0,2:T(8,128)} %copy.15, s32[160]{0:T(256)S(1)} %bitcast.46), kind=kOutput, calls=%fused_computation.4 | convolution fusion | flops 2013271040 | bytes 25166464 | tf_op jit(solution)/shard_map/st,sah->tah/dot_general | solution.py:52
  160.6 0.0 copy-start.2
  160.6 0.0 copy-start.5
  160.6 4.4 copy.12
  165.0 0.0 reduce-scatter.3.cloned.1.call-update
  165.0 0.0 all-gather.5.cloned.1.call-start
  165.0 0.2 convolution_bitcast_fusion.2
  165.2 72.3 %psum.28 = f32[4096]{0:T(1024)S(1)} all-reduce(f32[4096]{0:T(1024)S(1)} %convolution_bitcast_fusion.2), channel_id=1, replica_groups=mesh['row'=16,'col'=16] {'col'}, use_global_device_ids=true, to_apply=%region_1.0 | all-reduce | flops 4096 | bytes 32768 | tf_op jit(solution)/shard_map/psum | solution.py:36
  237.5 0.1 fusion.24
  237.6 27.1 %reduce-scatter.3.cloned.1.call-done = f32[256,256]{1,0:T(8,128)} async-done(((f32[4096,256]{1,0:T(8,128)}), f32[256,256]{1,0:T(8,128)}) %reduce-scatter.3.cloned.1.call-update) | async-done | bytes 262160 | tf_op jit(solution)/shard_map/reduce_scatter | solution.py:51
  264.7 1.8 fusion.26
  266.5 0.8 multiply_convert_fusion
  267.2 0.0 all-gather.5.cloned.1.call-update
  267.3 0.0 reduce-scatter.5.cloned.1.call-start
  267.3 58.2 %all-gather.5.cloned.1.call-done = bf16[4096,256]{1,0:T(8,128)(2,1)} async-done(((bf16[256,256]{1,0:T(8,128)(2,1)}), bf16[4096,256]{1,0:T(8,128)(2,1)}) %all-gather.5.cloned.1.call-update) | async-done | bytes 2097168 | tf_op jit(solution)/shard_map/all_gather | solution.py:65
  325.6 9.5 %gather_fusion.1 = bf16[160,128,256]{2,1,0:T(8,128)(2,1)} fusion(bf16[32,128,256]{2,1,0:T(8,128)(2,1)} %bitcast.43, s32[1024]{0:T(1024)S(1)} %pad_clamp_fusion), kind=kCustom, calls=%fused_computation.1 | custom fusion | bytes 20972160 | tf_op jit(solution)/shard_map/gather | solution.py:66
  335.1 14.4 %fusion.7 = f32[160,256,128]{2,1,0:T(8,128)} fusion(bf16[160,128,256]{2,1,0:T(8,128)(2,1)} %gather_fusion.1, s32[1,1,160,128,128]{4,3,2,1,0:T(8,128)} %param.13), kind=kOutput, calls=%fused_computation.10 | convolution fusion | flops 1344798720 | bytes 41943040 | tf_op jit(solution)/shard_map/sab,sah->sbh/dot_general | solution.py:67
  349.5 21.4 %copy.16 = f32[160,256,128]{1,0,2:T(8,128)} copy(f32[160,256,128]{2,1,0:T(8,128)} %fusion.7) | data formatting | bytes 41943040 | tf_op jit(solution)/shard_map/sab,sah->sbh/dot_general | solution.py:67
  370.9 11.7 %fusion = f32[32,128,256]{2,0,1:T(8,128)S(1)} fusion(f32[160,256,128]{1,0,2:T(8,128)} %copy.16, s32[160]{0:T(256)S(1)} %bitcast.49), kind=kOutput, calls=%fused_computation.2 | convolution fusion | flops 2013271040 | bytes 25166464 | tf_op jit(solution)/shard_map/st,sbh->tbh/dot_general | solution.py:70
  382.6 0.0 copy-start.1
  382.6 4.4 copy.13
  387.0 0.0 reduce-scatter.5.cloned.1.call-update
  387.0 0.0 all-reduce.2.cloned.1.call-start
  387.1 0.1 dynamic_slice.7
  387.1 76.0 %psum.31 = f32[256]{0:T(256)S(1)} all-reduce(f32[256]{0:T(256)S(1)} %get-tuple-element.14), channel_id=1, replica_groups=mesh['row'=16,'col'=16] {'row','col'}, use_global_device_ids=true, to_apply=%region_8.0 | all-reduce | flops 256 | bytes 2048 | tf_op jit(solution)/shard_map/psum | solution.py:82
  463.1 0.6 broadcast_multiply_fusion.1
  463.7 2.1 convolution_bitcast_fusion
  465.8 0.0 all-reduce.2.cloned.1.call-update
  465.8 1.9 convolution_convert_fusion
  467.7 235.2 %all-reduce.2.cloned.1.call-done = f32[128,256]{0,1:T(8,128)} async-done(((f32[128,256]{0,1:T(8,128)}), f32[128,256]{0,1:T(8,128)}) %all-reduce.2.cloned.1.call-update) | async-done | bytes 131088 | tf_op jit(solution)/shard_map/psum | solution.py:82
  702.9 0.9 broadcast_multiply_fusion
  703.8 0.8 copy.14
  (10 shorter events, 0.0 us)
Async XLA Ops:
  7.2 61.5 %copy-start = (bf16[128,256]{1,0:T(8,128)(2,1)S(1)}, bf16[128,256]{1,0:T(8,128)(2,1)}, u32[]{:S(2)}) copy-start(bf16[128,256]{1,0:T(8,128)(2,1)} %param.8) | copy-start | bytes 196612
  7.2 7.6 %copy-start.4 = (s32[1,1,160]{2,1,0:T(1,128)S(1)}, s32[1,1,160]{2,1,0:T(1,128)}, u32[]{:S(2)}) copy-start(s32[1,1,160]{2,1,0:T(1,128)} %param.12) | copy-start | bytes 1924
  7.2 61.4 %all-gather.3.cloned.1.call-start = ((), (), s32[]{:S(2)}) async-start(), calls=%async_computation.2 | async-start | bytes 1114112 | tf_op jit(solution)/shard_map/all_gather | solution.py:44
  7.9 256.7 %reduce-scatter.3.cloned.1.call-start = ((), (), s32[]{:S(2)}) async-start(), calls=%async_computation.3 | async-start | bytes 4456448 | tf_op jit(solution)/shard_map/reduce_scatter | solution.py:51
  127.5 21.3 %copy-start.3 = (s32[1,1,160]{2,1,0:T(1,128)S(1)}, s32[1,1,160]{2,1,0:T(1,128)}, u32[]{:S(2)}) copy-start(s32[1,1,160]{2,1,0:T(1,128)} %param.11) | copy-start | bytes 1924
  160.6 104.1 %copy-start.2 = (bf16[256,256]{1,0:T(8,128)(2,1)S(1)}, bf16[256,256]{1,0:T(8,128)(2,1)}, u32[]{:S(2)}) copy-start(bf16[256,256]{1,0:T(8,128)(2,1)} %param.10) | copy-start | bytes 393220
  160.6 104.1 %copy-start.5 = (f32[256]{0:T(256)S(1)}, f32[256]{0:T(256)}, u32[]{:S(2)}) copy-start(f32[256]{0:T(256)} %param.9) | copy-start | bytes 3076
  165.0 160.6 %all-gather.5.cloned.1.call-start = ((), (), s32[]{:S(2)}) async-start(), calls=%async_computation.4 | async-start | bytes 2228224 | tf_op jit(solution)/shard_map/all_gather | solution.py:65
  267.3 196.5 %reduce-scatter.5.cloned.1.call-start = ((), (), s32[]{:S(2)}) async-start(), calls=%async_computation.5 | async-start | bytes 4456448 | tf_op jit(solution)/shard_map/reduce_scatter | solution.py:73
  382.6 81.1 %copy-start.1 = (bf16[256,128]{1,0:T(8,128)(2,1)S(1)}, bf16[256,128]{1,0:T(8,128)(2,1)}, u32[]{:S(2)}) copy-start(bf16[256,128]{1,0:T(8,128)(2,1)} %param.7) | copy-start | bytes 196612
  387.0 315.9 %all-reduce.2.cloned.1.call-start = ((), (), s32[]{:S(2)}) async-start(), calls=%async_computation.6 | async-start | bytes 262144 | tf_op jit(solution)/shard_map/psum | solution.py:82
Sparse Core Ops, SparseCore 0:
  9.9 39.2 all-gather.2
  165.1 99.5 reduce-scatter.2
  268.0 57.5 all-gather.4
  387.1 64.3 reduce-scatter.4
  465.9 236.9 all-reduce.1
where the time goes:
time: 712 us; the launch traced here: 711 us
  waiting for transfers between devices  321 us (45%)
  blocking collectives  202 us (28%)
  matrix products  87.8 us (12%)
  local copies, waits for them, and re-layouts  75.1 us (11%)
  between operations  13.9 us (2%)
  other arithmetic  10.9 us (2%)
    psum x1, waiting for transfers between devices, on_device(): lax.psum((weight_term, bias_term), ('row', 'col'))  235 us
    psum x1, blocking collectives, on_device(): lax.psum((weight_term, bias_term), ('row', 'col'))  76 us
    psum x1, blocking collectives, on_device(): row_count = lax.psum(row_part, 'col')  72.3 us
    all_gather x1, waiting for transfers between devices, on_device(): gathered = lax.all_gather(sent, 'col', axis=0, tiled=True)  58.2 us
    psum x1, blocking collectives, on_device(): col_count = lax.psum(col_part, 'row')  53.7 us
    dot_general x1, matrix products, on_device(): jnp.einsum('sab,sbh->sah', entry_wide, picked, precision=lax.Precision.HI...  41.7 us
    reduce_scatter x1, waiting for transfers between devices, on_device(): lax.psum_scatter(jnp.einsum('st,sah->tah', onehot_rows, products, precisi...  27.1 us
    dot_general x1, local copies, waits for them, and re-layouts, on_device(): jnp.einsum('sab,sah->sbh', tile_values, picked_back, preferred_element_ty...  21.4 us
  transfers between devices with their start and end apart: 5, of which 3 were waited for; matrix products, arithmetic and copies ran while one was open for 1% of the time, Pallas kernels for 0%

commit v1 on v0

v1 whole, which is shorter than its diff:
```python
import functools

import jax
import jax.numpy as jnp
from jax import lax
from jax.experimental import pallas as pl
from jax.experimental.pallas import tpu as pltpu
from jax.sharding import PartitionSpec as P

F32 = jnp.float32
BF16 = jnp.bfloat16
T = 128
SLOTS = 160
CHUNK = 16
VMEM_LIMIT = 40 * 1024 * 1024
ROW_STEPS = tuple((dz, dy) for dz in range(2) for dy in range(4) if (dz, dy) != (0, 0))


def send(src, dst, send_sem, recv_sem, row, col):
    return pltpu.make_async_remote_copy(
        src_ref=src,
        dst_ref=dst,
        send_sem=send_sem,
        recv_sem=recv_sem,
        device_id=(row, col),
        device_id_type=pl.DeviceIdType.MESH,
    )


def row_place():
    row = lax.axis_index("row")
    return row // 8, (row // 2) % 4, row % 2


def row_at(zl, y, core):
    return zl * 8 + y * 2 + core


def greet(devices):
    barrier = pltpu.get_barrier_semaphore()
    for row, col in devices:
        pl.semaphore_signal(
            barrier, inc=1, device_id=(row, col), device_id_type=pl.DeviceIdType.MESH
        )
    pl.semaphore_wait(barrier, len(devices))


def split_dot(a, b):
    hi = a.astype(BF16)
    lo = (a - hi.astype(F32)).astype(BF16)
    return jnp.dot(hi, b, preferred_element_type=F32) + jnp.dot(lo, b, preferred_element_type=F32)


def spread_kernel(
    feat, col_ids, mask, narrow_out, scaled_out, scale_out,
    mask_in, narrow, feats, sums, count, sib_count, pair, far_count,
    mask_sem, narrow_sem, f_send, f_recv, g_send, g_recv, c_send, c_recv,
):
    row, col = lax.axis_index("row"), lax.axis_index("col")
    zl, y, core = row_place()
    sibling = row_at(zl, y, 1 - core)
    to = [row_at((zl + dz) % 2, (y + dy) % 4, core) for dz, dy in ROW_STEPS]
    frm = [row_at((zl - dz + 2) % 2, (y - dy + 4) % 4, core) for dz, dy in ROW_STEPS]
    n = len(ROW_STEPS)
    chunks = SLOTS // CHUNK
    loads = []
    for c in range(chunks):
        span = pl.ds(c * CHUNK, CHUNK)
        load = pltpu.make_async_copy(mask.at[span], mask_in.at[span], mask_sem.at[c])
        load.start()
        loads.append(load)
    greet([(sibling, col)] + [(p, col) for p in to])
    own = [send(feat, feats.at[row], f_send.at[k], f_recv.at[k], to[k], col) for k in range(n)]
    own.append(send(feat, feats.at[row], f_send.at[n], f_recv.at[n], sibling, col))
    for copy in own:
        copy.start()
    feats[row] = feat[...]
    stores = []
    for c in range(chunks):
        loads[c].wait()

        def eight(g, carry):
            at = pl.multiple_of(c * CHUNK + g * 8, 8)
            wide = mask_in[pl.ds(at, 8)].astype(F32)
            narrow[pl.ds(at, 8)] = wide.astype(BF16)
            sums[pl.ds(at, 8), :] = jnp.sum(wide, axis=1)
            return carry

        lax.fori_loop(0, CHUNK // 8, eight, 0)
        span = pl.ds(c * CHUNK, CHUNK)
        store = pltpu.make_async_copy(narrow.at[span], narrow_out.at[span], narrow_sem.at[c])
        store.start()
        stores.append(store)
    onehot = (lax.broadcasted_iota(jnp.int32, (32, SLOTS), 0) == col_ids[...]).astype(BF16)
    count[...] = jnp.dot(onehot, sums[...].astype(BF16), preferred_element_type=F32)
    near = send(count, sib_count, c_send.at[n], c_recv.at[n], sibling, col)
    near.start()
    forwards = []
    for k in range(n):
        own[k].wait_recv()
        block = feats.at[frm[k]]
        forward = send(block, block, g_send.at[k], g_recv.at[k], sibling, col)
        forward.start()
        forwards.append(forward)
    near.wait()
    pair[...] = count[...] + sib_count[...]
    far = [send(pair, far_count.at[k], c_send.at[k], c_recv.at[k], to[k], col) for k in range(n)]
    for copy in far:
        copy.start()
    total = pair[...]
    for k in range(n):
        far[k].wait_recv()
        total = total + far_count[k]
    scale = 1.0 / jnp.sqrt(1.0 + total)
    scale_out[...] = scale
    turned = jnp.transpose(jnp.concatenate([scale, jnp.zeros((96, T), F32)], axis=0))
    own[n].wait_recv()
    for k in range(n):
        forwards[k].wait_recv()
    for t in range(32):
        block = feats[t // 2, pl.ds((t % 2) * T, T), :].astype(F32)
        scaled_out[t] = (block * turned[:, t:t + 1]).astype(BF16)
    for copy in own + forwards + far:
        copy.wait_send()
    for store in stores:
        store.wait()


def forward_kernel(row_ids, col_ids, narrow, scaled, out, count_out, acc, hits):
    step = pl.program_id(0)

    @pl.when(step == 0)
    def _():
        acc[...] = jnp.zeros_like(acc)
        hits[...] = jnp.zeros_like(hits)

    for g in range(CHUNK // 4):
        terms = []
        for i in range(4):
            s = g * 4 + i
            terms.append(
                jnp.dot(narrow[s], scaled[col_ids[step * CHUNK + s]], preferred_element_type=F32)
            )
        for i in range(4):
            s = g * 4 + i
            r = row_ids[step * CHUNK + s]
            acc[r] += terms[i]
            hits[r] += narrow[s]

    @pl.when(step == pl.num_programs(0) - 1)
    def _():
        out[...] = acc[...].astype(BF16)
        ones = jnp.ones((8, T), BF16)
        for t in range(32):
            row_sum = lax.dot_general(
                ones, hits[t], (((1,), (1,)), ((), ())), preferred_element_type=F32
            )
            count_out[pl.ds(t, 1), :] = row_sum[0:1]


def middle_kernel(
    part, row_part, weight, bias, cot,
    act_out, back_out, grad_out,
    x_in, x_sum, z_in, cx_in, c_sum, cz_in, grads, gx_in, gz_buf, gz_in, back,
    xs, xr, zs, zr, cxs, cxr, czs, czr, gxs, gxr, gzs, gzr, hzs, hzr, hxs, hxr, local_sem,
):
    row, col = lax.axis_index("row"), lax.axis_index("col")
    x, z = col // 4, col % 4

    def x_to(d):
        return (x + d) % 4

    def z_to(d):
        return (z + d) % 4

    peers_x = [x_to(d) * 4 + z for d in (1, 2, 3)]
    peers_z = [x * 4 + z_to(d) for d in (1, 2, 3)]
    greet([(row, p) for p in peers_x + peers_z])
    cx = []
    for k in range(3):
        cx.append(send(row_part.at[x_to(k + 1)], cx_in.at[k], cxs.at[k], cxr.at[k], row, peers_x[k]))
        cx[k].start()
    order = (2, 1, 3, 0)
    sends_x = {}
    for e in order:
        zc = z_to(e)
        for k in (1, 0, 2):
            copy = send(
                part.at[x_to(k + 1) * 4 + zc], x_in.at[k, e], xs.at[k, e], xr.at[k, e],
                row, peers_x[k],
            )
            copy.start()
            sends_x[k, e] = copy
    total_count = row_part[x]
    for k in range(3):
        cx[k].wait_recv()
        total_count = total_count + cx_in[k]
    c_sum[...] = total_count
    cz = []
    for k in range(3):
        cz.append(send(c_sum, cz_in.at[k], czs.at[k], czr.at[k], row, peers_z[k]))
        cz[k].start()
    sends_z = []
    agg = None
    for e in order:
        for k in range(3):
            sends_x[k, e].wait_recv()
        total = part[x * 4 + z_to(e)].astype(F32)
        for k in range(3):
            total = total + x_in[k, e].astype(F32)
        if e == 0:
            agg = total
        else:
            x_sum[e - 1] = total.astype(BF16)
            copy = send(x_sum.at[e - 1], z_in.at[e - 1], zs.at[e - 1], zr.at[e - 1], row, peers_z[e - 1])
            copy.start()
            sends_z.append(copy)
    total_count = c_sum[...]
    for k in range(3):
        cz[k].wait_recv()
        total_count = total_count + cz_in[k]
    cx_in[0] = 1.0 / jnp.sqrt(1.0 + total_count)
    turned = [
        jnp.transpose(jnp.broadcast_to(cx_in[0, pl.ds(2 * z + h, 1), :], (T, T))) for h in range(2)
    ]
    scale = jnp.concatenate(turned, axis=0)
    scale = jnp.concatenate([scale, scale], axis=1)
    for copy in sends_z:
        copy.wait_recv()
    for k in range(3):
        agg = agg + z_in[k].astype(F32)
    summed = split_dot(agg, weight[...])
    pre = scale * summed + bias[...]
    sig = jax.nn.sigmoid(pre)
    act_out[...] = (pre * sig).astype(BF16)
    grad_pre = cot[...].astype(F32) * sig * (1.0 + pre * (1.0 - sig))
    sent = (scale * grad_pre).astype(BF16)
    turned_back = lax.dot_general(
        weight[...], sent, (((1,), (1,)), ((), ())), preferred_element_type=F32
    ).astype(BF16)
    back[0] = turned_back[:, :T]
    back[1] = turned_back[:, T:]
    mine = back_out.at[col]
    keep = pltpu.make_async_copy(back, mine, local_sem)
    keep.start()
    hz, hx = [], []
    for k in range(3):
        hz.append(send(back, mine, hzs.at[k], hzr.at[k], row, peers_z[k]))
        hz[k].start()
    for k in (1, 0, 2):
        copy = send(back, mine, hxs.at[k, 0], hxr.at[k, 0], row, peers_x[k])
        copy.start()
        hx.append(copy)
    weight_term = split_dot(jnp.transpose(agg), sent)
    bias_term = jnp.broadcast_to(jnp.sum(grad_pre, axis=0, keepdims=True), (8, 256))
    for c in range(4):
        for e in range(4):
            at = (c * 4 + e) * 8
            grads[c, e] = weight_term[at:at + 8]
        grads[c, 4] = bias_term
    gx = []
    for k in range(3):
        gx.append(send(grads.at[x_to(k + 1)], gx_in.at[k], gxs.at[k], gxr.at[k], row, peers_x[k]))
        gx[k].start()
    for k in range(3):
        hz[k].wait_recv()
        src = back_out.at[x * 4 + (z - k - 1 + 4) % 4]
        for j in (1, 0, 2):
            copy = send(src, src, hxs.at[j, k + 1], hxr.at[j, k + 1], row, peers_x[j])
            copy.start()
            hx.append(copy)
    total = grads[x]
    for k in range(3):
        gx[k].wait_recv()
        total = total + gx_in[k]
    for e in range(4):
        gz_buf[e, 0] = total[e]
        gz_buf[e, 1] = total[4]
    gz = []
    for k in range(3):
        gz.append(send(gz_buf.at[z_to(k + 1)], gz_in.at[k], gzs.at[k], gzr.at[k], row, peers_z[k]))
        gz[k].start()
    total = gz_buf[z]
    for k in range(3):
        gz[k].wait_recv()
        total = total + gz_in[k]
    grad_out[...] = total
    for copy in hx:
        copy.wait_recv()
    keep.wait()
    for copy in cx + cz + list(sends_x.values()) + sends_z + hz + hx + gx + gz:
        copy.wait_send()


def backward_kernel(row_ids, col_ids, narrow, back, out, acc):
    step = pl.program_id(0)

    @pl.when(step == 0)
    def _():
        acc[...] = jnp.zeros_like(acc)

    for g in range(CHUNK // 4):
        terms = []
        for i in range(4):
            s = g * 4 + i
            terms.append(
                jnp.dot(back[row_ids[step * CHUNK + s]], narrow[s], preferred_element_type=F32)
            )
        for i in range(4):
            s = g * 4 + i
            acc[col_ids[step * CHUNK + s]] += terms[i]

    @pl.when(step == pl.num_programs(0) - 1)
    def _():
        out[...] = acc[...].astype(BF16)


def finish_kernel(
    factor, part, scale, grad,
    feat_out, weight_out, bias_out,
    sib_in, pair, far_in, gsib_in, gpair, gfar_in, gall,
    ss, sr, fs, fr, gss, gsr, gfs, gfr, gzs, gzr, gxs, gxr,
):
    row, col = lax.axis_index("row"), lax.axis_index("col")
    zl, y, core = row_place()
    x, z = col // 4, col % 4
    sibling = row_at(zl, y, 1 - core)
    to = [row_at((zl + dz) % 2, (y + dy) % 4, core) for dz, dy in ROW_STEPS]
    n = len(ROW_STEPS)
    peers_x = [((x + d) % 4) * 4 + z for d in (1, 2, 3)]
    peers_z = [x * 4 + (z + d) % 4 for d in (1, 2, 3)]
    greet(
        [(sibling, col)] + [(p, col) for p in to] + [(row, p) for p in peers_x + peers_z]
    )
    gnear = send(grad, gsib_in, gss, gsr, sibling, col)
    gnear.start()
    near = []
    for q in range(8):
        copy = send(part.at[q, 1 - core], sib_in.at[q], ss.at[q], sr.at[q], sibling, col)
        copy.start()
        near.append(copy)
    gnear.wait()
    gpair[...] = grad[...] + gsib_in[...]
    gfar = []
    for k in range(n):
        gfar.append(send(gpair, gfar_in.at[k], gfs.at[k], gfr.at[k], to[k], col))
        gfar[k].start()
    for copy in near:
        copy.wait()

    def pair_sum(q, carry):
        pair[q] = (part[q, core].astype(F32) + sib_in[q].astype(F32)).astype(BF16)
        return carry

    lax.fori_loop(0, 8, pair_sum, 0)
    far = []
    for k, (dz, dy) in enumerate(ROW_STEPS):
        q = ((zl + dz) % 2) * 4 + (y + dy) % 4
        far.append(send(pair.at[q], far_in.at[k], fs.at[k], fr.at[k], to[k], col))
        far[k].start()
    total = gpair[...]
    for k in range(n):
        gfar[k].wait_recv()
        total = total + gfar_in[k]
    total = total * factor
    gall[col] = total[0]
    bias_out[...] = total[1, 0:1]
    mine = gall.at[col]
    gz, gx = [], []
    for k in range(3):
        gz.append(send(mine, mine, gzs.at[k], gzr.at[k], row, peers_z[k]))
        gz[k].start()
    for k in range(3):
        gx.append(send(mine, mine, gxs.at[k, 0], gxr.at[k, 0], row, peers_x[k]))
        gx[k].start()
    for k in range(3):
        gz[k].wait_recv()
        src = gall.at[x * 4 + (z - k - 1 + 4) % 4]
        for j in range(3):
            copy = send(src, src, gxs.at[j, k + 1], gxr.at[j, k + 1], row, peers_x[j])
            copy.start()
            gx.append(copy)
    block = pair[zl * 4 + y].astype(F32)
    for k in range(n):
        far[k].wait_recv()
        block = block + far_in[k].astype(F32)
    for h in range(2):
        scaled = block[h] * scale[pl.ds(row * 2 + h, 1), :]
        feat_out[pl.ds(h * T, T), :] = jnp.transpose(scaled).astype(BF16)
    for copy in gx:
        copy.wait_recv()
    for c in range(16):
        weight_out[pl.ds(c * 8, 8), :] = gall[c]
    for copy in gfar + far + gz + gx:
        copy.wait_send()


def params(collective_id=None):
    if collective_id is None:
        return pltpu.CompilerParams(
            vmem_limit_bytes=VMEM_LIMIT, dimension_semantics=("arbitrary",)
        )
    return pltpu.CompilerParams(
        vmem_limit_bytes=VMEM_LIMIT, has_side_effects=True, collective_id=collective_id
    )


def on_device(features, weight, bias, cotangent, tile_rows, tile_cols, tile_mask):
    nodes = features.shape[0] * lax.axis_size("row") * lax.axis_size("col")
    row_ids = tile_rows.reshape(SLOTS)
    col_ids = tile_cols.reshape(SLOTS)
    mask = tile_mask.reshape(SLOTS, T, T)
    vmem = pl.BlockSpec(memory_space=pltpu.VMEM)
    hbm = pl.BlockSpec(memory_space=pl.ANY)
    dma = pltpu.SemaphoreType.DMA
    shape = jax.ShapeDtypeStruct
    n = len(ROW_STEPS)
    chunks = SLOTS // CHUNK

    narrow, scaled, scale = pl.pallas_call(
        spread_kernel,
        out_shape=(
            shape((SLOTS, T, T), BF16),
            shape((32, T, T), BF16),
            shape((32, T), F32),
        ),
        in_specs=[vmem, vmem, hbm],
        out_specs=(hbm, vmem, vmem),
        scratch_shapes=[
            pltpu.VMEM((SLOTS, T, T), jnp.int32),
            pltpu.VMEM((SLOTS, T, T), BF16),
            pltpu.VMEM((16, 256, T), BF16),
            pltpu.VMEM((SLOTS, T), F32),
            pltpu.VMEM((32, T), F32),
            pltpu.VMEM((32, T), F32),
            pltpu.VMEM((32, T), F32),
            pltpu.VMEM((n, 32, T), F32),
            dma((chunks,)), dma((chunks,)),
            dma((n + 1,)), dma((n + 1,)), dma((n,)), dma((n,)), dma((n + 1,)), dma((n + 1,)),
        ],
        compiler_params=params(1),
        name="spread",
    )(features, col_ids.reshape(1, SLOTS), mask)

    tile_block = pl.BlockSpec((CHUNK, T, T), lambda i, *_: (i, 0, 0))
    whole = pl.BlockSpec((32, T, T), lambda i, *_: (0, 0, 0))
    part, row_part = pl.pallas_call(
        forward_kernel,
        out_shape=(shape((32, T, T), BF16), shape((32, T), F32)),
        grid_spec=pltpu.PrefetchScalarGridSpec(
            num_scalar_prefetch=2,
            grid=(chunks,),
            in_specs=[tile_block, whole],
            out_specs=[whole, pl.BlockSpec((32, T), lambda i, *_: (0, 0))],
            scratch_shapes=[pltpu.VMEM((32, T, T), F32), pltpu.VMEM((32, T, T), BF16)],
        ),
        compiler_params=params(),
        name="forward",
    )(row_ids, col_ids, narrow, scaled)

    activations, back, grad_part = pl.pallas_call(
        middle_kernel,
        out_shape=(
            shape((256, 256), BF16),
            shape((16, 2, T, T), BF16),
            shape((2, 8, 256), F32),
        ),
        in_specs=[vmem] * 5,
        out_specs=(vmem, hbm, vmem),
        scratch_shapes=[
            pltpu.VMEM((3, 4, 256, T), BF16),
            pltpu.VMEM((3, 256, T), BF16),
            pltpu.VMEM((3, 256, T), BF16),
            pltpu.VMEM((3, 8, T), F32),
            pltpu.VMEM((8, T), F32),
            pltpu.VMEM((3, 8, T), F32),
            pltpu.VMEM((4, 5, 8, 256), F32),
            pltpu.VMEM((3, 5, 8, 256), F32),
            pltpu.VMEM((4, 2, 8, 256), F32),
            pltpu.VMEM((3, 2, 8, 256), F32),
            pltpu.VMEM((2, T, T), BF16),
            dma((3, 4)), dma((3, 4)), dma((3,)), dma((3,)),
            dma((3,)), dma((3,)), dma((3,)), dma((3,)),
            dma((3,)), dma((3,)), dma((3,)), dma((3,)),
            dma((3,)), dma((3,)), dma((3, 4)), dma((3, 4)),
            dma,
        ],
        compiler_params=params(2),
        name="middle",
    )(part.reshape(16, 256, T), row_part.reshape(4, 8, T), weight, bias.reshape(1, 256), cotangent)

    column_part = pl.pallas_call(
        backward_kernel,
        out_shape=shape((32, T, T), BF16),
        grid_spec=pltpu.PrefetchScalarGridSpec(
            num_scalar_prefetch=2,
            grid=(chunks,),
            in_specs=[tile_block, whole],
            out_specs=whole,
            scratch_shapes=[pltpu.VMEM((32, T, T), F32)],
        ),
        compiler_params=params(),
        name="backward",
    )(row_ids, col_ids, narrow, back.reshape(32, T, T))

    factor = 1.0 / float(nodes) ** 0.5
    grad_features, grad_weight, grad_bias = pl.pallas_call(
        functools.partial(finish_kernel, factor),
        out_shape=(
            shape((256, T), BF16),
            shape((T, 256), F32),
            shape((1, 256), F32),
        ),
        in_specs=[vmem] * 3,
        out_specs=(vmem, vmem, vmem),
        scratch_shapes=[
            pltpu.VMEM((8, 2, T, T), BF16),
            pltpu.VMEM((8, 2, T, T), BF16),
            pltpu.VMEM((n, 2, T, T), BF16),
            pltpu.VMEM((2, 8, 256), F32),
            pltpu.VMEM((2, 8, 256), F32),
            pltpu.VMEM((n, 2, 8, 256), F32),
            pltpu.VMEM((16, 8, 256), F32),
            dma((8,)), dma((8,)), dma((n,)), dma((n,)),
            dma, dma, dma((n,)), dma((n,)),
            dma((3,)), dma((3,)), dma((3, 4)), dma((3, 4)),
        ],
        compiler_params=params(3),
        name="finish",
    )(column_part.reshape(8, 2, 2, T, T), scale, grad_part)
    return (activations, grad_features, grad_weight, grad_bias.reshape(256))


def solution(mesh):
    placed = (
        P(("col", "row"), None),
        P(),
        P(),
        P(("row", "col"), None),
        P("row", "col", None),
        P("row", "col", None),
        P("row", "col", None, None, None),
    )
    return jax.shard_map(
        on_device,
        mesh=mesh,
        in_specs=placed,
        out_specs=(P(("row", "col"), None), P(("col", "row"), None), P(), P()),
        check_vma=False,
    )
```

time: 712 us -> 91.4 us (0.13)
  waiting for transfers between devices: 321 us -> 0 us
  blocking collectives: 202 us -> 0 us
  matrix products: 87.8 us -> 0 us
  Pallas kernels: 0 us -> 86.5 us
  local copies, waits for them, and re-layouts: 75.1 us -> 4.09 us
  between operations: 13.9 us -> 0.71 us
  other arithmetic: 10.9 us -> 0 us
    psum x1 -> x0, waiting for transfers between devices: 235 us -> none  [on_device(): lax.psum((weight_term, bias_term), ('row', 'col'))]
    psum x3 -> x0, blocking collectives: 202 us -> none  [the longest x1 76 us: on_device(): lax.psum((weight_term, bias_term), ('row', 'col'))]
    dot_general x9 -> x0, matrix products: 87.8 us -> none  [the longest x1 41.7 us: on_device(): jnp.einsum('sab,sbh->sah', entry_wide, picked, precision=lax.Precision.HI...]
    pallas_call x0 -> x5, Pallas kernels: none -> 86.5 us  [the longest x1 32.8 us: on_device(): pl.pallas_call(middle_kernel, out_shape=(shape((256, 256), BF16), shape((...]
    all_gather x2 -> x0, waiting for transfers between devices: 58.3 us -> none  [the longest x1 58.2 us: on_device(): gathered = lax.all_gather(sent, 'col', axis=0, tiled=True)]
    dot_general x4 -> x0, local copies, waits for them, and re-layouts: 51.4 us -> none  [the longest x1 21.4 us: on_device(): jnp.einsum('sab,sah->sbh', tile_values, picked_back, preferred_element_ty...]
    reduce_scatter x2 -> x0, waiting for transfers between devices: 27.1 us -> none  [the longest x1 27.1 us: on_device(): lax.psum_scatter(jnp.einsum('st,sah->tah', onehot_rows, products, precisi...]
    gather x2 -> x0, local copies, waits for them, and re-layouts: 22.8 us -> none  [the longest x1 13.3 us: on_device(): picked = scaled.reshape(col_tiles, 128, width)[col_ids]]
  transfers between devices with their start and end apart: 5 -> 0, of which waited for: 3 -> 0; matrix products, arithmetic and copies ran while one was open for 1% -> 0% of each run, Pallas kernels for 0% -> 0%
where the time goes in v1:
time: 91.4 us; the launch traced here: 91.3 us
  Pallas kernels  86.5 us (95%)
  local copies, waits for them, and re-layouts  4.09 us (4%)
    pallas_call x1, Pallas kernels, on_device(): pl.pallas_call(middle_kernel, out_shape=(shape((256, 256), BF16), shape((...  32.8 us
    pallas_call x1, Pallas kernels, on_device(): pl.pallas_call(functools.partial(finish_kernel, factor), out_shape=(shape...  26.8 us
    pallas_call x1, Pallas kernels, on_device(): pl.pallas_call(spread_kernel, out_shape=(shape((SLOTS, T, T), BF16), shap...  17.4 us
    pallas_call x1, Pallas kernels, on_device(): pl.pallas_call(forward_kernel, out_shape=(shape((32, T, T), BF16), shape(...  5.45 us
    unnamed x18, local copies, waits for them, and re-layouts  4.09 us
    pallas_call x1, Pallas kernels, on_device(): pl.pallas_call(backward_kernel, out_shape=shape((32, T, T), BF16), grid_s...  4.01 us

profile of v1, /device:TPU:1, one launch (start us, length us, event | category | flops | bytes accessed | tf_op | source)
XLA Modules:
  0.0 91.3 jit_solution(1225439303759142199)
XLA Ops:
  0.6 0.0 copy-start
  0.6 0.0 copy-start.1
  0.7 0.9 copy-done.1
  1.5 0.0 copy-start.3
  1.5 0.7 copy-done.3
  2.2 0.0 copy-start.5
  2.2 0.0 copy-start.2
  2.2 0.0 copy-start.6
  2.2 0.0 copy-start.4
  2.2 17.4 %spread.1 = (bf16[160,128,128]{2,1,0:T(8,128)(2,1)S(1)}, bf16[32,128,128]{2,1,0:T(8,128)(2,1)S(1)}, f32[32,128]{1,0:T(8,128)S(1)}) custom-call(bf16[256,128]{1,0:T(8,128)(2,1)S(1)} %copy-done.1, s32[1,160]{1,0:T(1,128)S(1)} %bitcast.14, s32[160,128,128]{2,1,0:T(8,128)} %bitcast.21), custom_call_target="tpu_custom_call" | custom-call | tf_op jit(solution)/shard_map/spread/pallas_call | solution.py:420
  19.6 0.0 copy-done.5
  19.6 5.5 %forward.1 = (bf16[32,128,128]{2,1,0:T(8,128)(2,1)S(1)}, f32[32,128]{1,0:T(8,128)S(1)}) custom-call(s32[160]{0:T(256)S(1)} %bitcast.17, s32[160]{0:T(256)S(1)} %bitcast.15, bf16[160,128,128]{2,1,0:T(8,128)(2,1)S(1)} %get-tuple-element.15.narrow, bf16[32,128,128]{2,1,0:T(8,128)(2,1)S(1)} %get-tuple-element.16.scaled), custom_call_target="tpu_custom_call" | custom-call | tf_op jit(solution)/shard_map/forward/pallas_call | solution.py:447
  25.1 0.0 copy-done
  25.1 0.0 copy-done.2
  25.1 0.0 copy-done.6
  25.1 32.8 %middle.1 = (bf16[256,256]{1,0:T(8,128)(2,1)S(1)}, bf16[16,2,128,128]{3,2,1,0:T(8,128)(2,1)S(1)}, f32[2,8,256]{2,1,0:T(8,128)S(1)}) custom-call(bf16[16,256,128]{2,1,0:T(8,128)(2,1)S(1)} %bitcast.11, f32[4,8,128]{2,1,0:T(8,128)S(1)} %bitcast.13, bf16[128,256]{1,0:T(8,128)(2,1)S(1)} %copy-done.2, f32[1,256]{1,0:T(1,128)S(1)} %bitcast.20, ...), custom_call_target="tpu_custom_call" | custom-call | tf_op jit(solution)/shard_map/middle/pallas_call | solution.py:461
  57.9 0.0 copy-done.4
  57.9 4.0 %backward.1 = bf16[32,128,128]{2,1,0:T(8,128)(2,1)S(1)} custom-call(s32[160]{0:T(256)S(1)} %bitcast.18, s32[160]{0:T(256)S(1)} %bitcast.16, bf16[160,128,128]{2,1,0:T(8,128)(2,1)S(1)} %get-tuple-element.15.narrow, bf16[32,128,128]{2,1,0:T(8,128)(2,1)S(1)} %bitcast.12), custom_call_target="tpu_custom_call" | custom-call | tf_op jit(solution)/shard_map/backward/pallas_call | solution.py:492
  62.0 26.8 %finish.1 = (bf16[256,128]{1,0:T(8,128)(2,1)S(1)}, f32[128,256]{1,0:T(8,128)S(1)}, f32[1,256]{1,0:T(1,128)S(1)}) custom-call(bf16[8,2,2,128,128]{4,3,2,1,0:T(8,128)(2,1)S(1)} %bitcast.10, f32[32,128]{1,0:T(8,128)S(1)} %get-tuple-element.21.scale, f32[2,8,256]{2,1,0:T(8,128)S(1)} %get-tuple-element.22.grad), custom_call_target="tpu_custom_call" | custom-call | tf_op jit(solution)/shard_map/finish/pallas_call | solution.py:507
  88.8 0.7 copy.15
  89.4 0.6 copy.16
  90.1 0.7 copy.17
  90.7 0.6 copy.18
Async XLA Ops:
  0.6 24.4 %copy-start = (bf16[256,256]{1,0:T(8,128)(2,1)S(1)}, bf16[256,256]{1,0:T(8,128)(2,1)}, u32[]{:S(2)}) copy-start(bf16[256,256]{1,0:T(8,128)(2,1)} %cot.1) | copy-start | bytes 393220
  0.6 0.9 copy-start.1
  1.5 0.7 copy-start.3
  2.2 17.4 %copy-start.5 = (s32[1,1,160]{2,1,0:T(1,128)S(1)}, s32[1,1,160]{2,1,0:T(1,128)}, u32[]{:S(2)}) copy-start(s32[1,1,160]{2,1,0:T(1,128)} %param.11) | copy-start | bytes 1924
  2.2 22.9 %copy-start.2 = (bf16[128,256]{1,0:T(8,128)(2,1)S(1)}, bf16[128,256]{1,0:T(8,128)(2,1)}, u32[]{:S(2)}) copy-start(bf16[128,256]{1,0:T(8,128)(2,1)} %weight.1) | copy-start | bytes 196612
  2.2 22.9 %copy-start.6 = (f32[256]{0:T(256)S(1)}, f32[256]{0:T(256)}, u32[]{:S(2)}) copy-start(f32[256]{0:T(256)} %param.9) | copy-start | bytes 3076
  2.2 55.7 %copy-start.4 = (s32[1,1,160]{2,1,0:T(1,128)S(1)}, s32[1,1,160]{2,1,0:T(1,128)}, u32[]{:S(2)}) copy-start(s32[1,1,160]{2,1,0:T(1,128)} %param.12) | copy-start | bytes 1924

commit v2 on v0

v2 whole, which is shorter than its diff:
```python
import functools

import jax
import jax.numpy as jnp
from jax import lax
from jax.experimental import pallas as pl
from jax.experimental.pallas import tpu as pltpu
from jax.sharding import PartitionSpec as P

F32 = jnp.float32
BF16 = jnp.bfloat16
T = 128
SLOTS = 160
CHUNK = 16
GROUP = 16
PAIRS = (SLOTS + 32) // 2
COPIES = 102
VMEM_LIMIT = 56 * 1024 * 1024
ROW_STEPS = tuple((dz, dy) for dz in (1, 0) for dy in (2, 1, 3, 0) if (dz, dy) != (0, 0))
NEAR = (1, 0, 2)


class Links:
    def __init__(self, send_sems, recv_sems):
        self.send_sems, self.recv_sems = send_sems, recv_sems
        self.started = []

    def send(self, src, dst, device):
        k = len(self.started)
        copy = pltpu.make_async_remote_copy(
            src_ref=src,
            dst_ref=dst,
            send_sem=self.send_sems.at[k],
            recv_sem=self.recv_sems.at[k],
            device_id=device,
            device_id_type=pl.DeviceIdType.MESH,
        )
        copy.start()
        self.started.append(copy)
        return copy

    def drain(self):
        for copy in self.started:
            copy.wait_send()


def split_dot(a, b):
    hi = a.astype(BF16)
    lo = (a - hi.astype(F32)).astype(BF16)
    return jnp.dot(hi, b, preferred_element_type=F32) + jnp.dot(lo, b, preferred_element_type=F32)


def sort_lists(ids, others, lists, at):
    lane = lax.broadcasted_iota(jnp.int32, (1, 256), 1)
    key = (jnp.where(lane < SLOTS, ids, 64) * 256 + lane).astype(F32)
    along = jnp.broadcast_to(key, (256, 256))
    down = jnp.transpose(along)
    wide_lane = lax.broadcasted_iota(jnp.int32, (256, 256), 1).astype(F32)
    id_down = jnp.floor(down * (1.0 / 256.0))
    rank = jnp.sum((along < down).astype(F32), axis=1, keepdims=True)
    held = jnp.sum((id_down == wide_lane).astype(F32), axis=0, keepdims=True)
    odd = held - 2.0 * jnp.floor(held * 0.5)
    below = jnp.sum(jnp.where(wide_lane < id_down, odd, 0.0), axis=1, keepdims=True)
    pos = rank + below
    first = 1.0 - (pos - 2.0 * jnp.floor(pos * 0.5))
    place = jnp.where(id_down < 63.0, (pos == wide_lane).astype(F32), 0.0).astype(BF16)
    row = lax.broadcasted_iota(jnp.int32, (8, 256), 0)
    values = jnp.where(row == 0, lane + 1, jnp.where(row == 1, others, ids))
    moved = jnp.dot(values.astype(F32).astype(BF16), place, preferred_element_type=F32)
    upto = jnp.where(id_down <= wide_lane, first, 0.0)
    last = jnp.sum(upto, axis=0, keepdims=True) - 1.0
    found = jnp.where(row == 3, last, moved).astype(jnp.int32)
    least = jnp.where(row == 3, -1, 0)
    most = jnp.where(row == 0, SLOTS, jnp.where(row == 3, PAIRS - 1, 31))
    lists[pl.ds(at, 8), :] = jnp.minimum(jnp.maximum(found, least), most)


def layer_kernel(
    factor,
    feat, weight_hbm, bias_hbm, cot_hbm, row_hbm, col_hbm, mask,
    act_out, feat_out, weight_out, bias_out,
    weight, bias, cot, row_ids, col_ids,
    mask_in, narrow, running, padded, lists_v, lists,
    feats, sums, count, sib_count, pair_count, far_count,
    row_count, rx_in, rx_sum, rz_in, scaled,
    part, x_in, z_buf, z_in, back,
    scale_keep, row_scale, grads, gsib_in, gq_buf, gq_in, gx_buf, gz_buf, gall,
    col_part, sib_in, pair, far_in,
    mask_sem, list_sem, in_sem, send_sems, recv_sems,
):
    row, col = lax.axis_index("row"), lax.axis_index("col")
    zl, y, core = row // 8, (row // 2) % 4, row % 2
    x, z = col // 4, col % 4
    here = zl * 4 + y
    sibling = (zl * 8 + y * 2 + 1 - core, col)
    row_to = [(((zl + dz) % 2) * 8 + ((y + dy) % 4) * 2 + core, col) for dz, dy in ROW_STEPS]
    row_from = [((zl - dz + 2) % 2) * 4 + (y - dy + 4) % 4 for dz, dy in ROW_STEPS]
    far = len(ROW_STEPS)
    x_at = [(x + d) % 4 for d in (1, 2, 3)]
    z_at = [(z + d) % 4 for d in (1, 2, 3)]
    x_to = [(row, p * 4 + z) for p in x_at]
    z_to = [(row, x * 4 + p) for p in z_at]
    x_from = [(x - d + 4) % 4 for d in (1, 2, 3)]
    z_from = [(z - d + 4) % 4 for d in (1, 2, 3)]
    links = Links(send_sems, recv_sems)
    send = links.send

    barrier = pltpu.get_barrier_semaphore()
    peers = [sibling] + row_to + x_to + z_to
    for device in peers:
        pl.semaphore_signal(
            barrier, inc=1, device_id=device, device_id_type=pl.DeviceIdType.MESH
        )
    chunks = SLOTS // CHUNK
    loads = []
    held_in = []
    for k, (src, dst) in enumerate(
        (
            (row_hbm, row_ids),
            (col_hbm, col_ids),
            (feat, feats.at[core, here]),
            (weight_hbm, weight),
            (bias_hbm, bias),
            (cot_hbm, cot),
        )
    ):
        held_in.append(pltpu.make_async_copy(src, dst, in_sem.at[k]))
    for copy in held_in[:2]:
        copy.start()
    for c in range(chunks):
        span = pl.ds(c * CHUNK, CHUNK)
        load = pltpu.make_async_copy(mask.at[span], mask_in.at[span], mask_sem.at[c])
        load.start()
        loads.append(load)
        if c == 1:
            for copy in held_in[2:]:
                copy.start()

    narrow[0] = jnp.zeros((T, T), BF16)

    def take(c):
        loads[c].wait()

        def eight(g, carry):
            at = pl.multiple_of(c * CHUNK + g * 8, 8)
            wide = mask_in[pl.ds(at, 8)].astype(F32)
            narrow[pl.ds(at + 1, 8)] = wide.astype(BF16)
            sums[pl.ds(at, 8), :] = jnp.sum(wide, axis=1)
            return carry

        lax.fori_loop(0, CHUNK // 8, eight, 0)

    for c in range(chunks // 2):
        take(c)
    pl.semaphore_wait(barrier, len(peers))
    held_in[2].wait()
    mine = feats.at[core, here]
    own = [send(mine, mine, device) for device in row_to + [sibling]]
    for c in range(chunks // 2, chunks):
        take(c)
    slot_row = lax.broadcasted_iota(jnp.int32, (32, SLOTS), 0)
    for copy in held_in[:2]:
        copy.wait()
    onehot = (slot_row == col_ids[...]).astype(BF16)
    count[...] = jnp.dot(onehot, sums[...].astype(BF16), preferred_element_type=F32)
    near = send(count, sib_count, sibling)

    near.wait_recv()
    pair_count[...] = count[...] + sib_count[...]
    far_counts = [send(pair_count, far_count.at[k], row_to[k]) for k in range(far)]
    padded[...] = jnp.zeros_like(padded)
    padded[0:1, 0:SLOTS] = row_ids[...]
    padded[8:9, 0:SLOTS] = col_ids[...]
    rows_wide, cols_wide = padded[0:1, :], padded[8:9, :]
    sort_lists(rows_wide, cols_wide, lists_v, 0)
    sort_lists(cols_wide, rows_wide, lists_v, 8)
    list_copy = pltpu.make_async_copy(lists_v, lists, list_sem)
    list_copy.start()
    ones = jnp.ones((8, T), BF16)

    def row_sums(g, carry):
        at = pl.multiple_of(g * 8, 8)
        tiles = narrow[pl.ds(at + 1, 8)].reshape(8 * T, T)
        got = lax.dot_general(ones, tiles, (((1,), (1,)), ((), ())), preferred_element_type=F32)
        sums[pl.ds(at, 8), :] = jnp.concatenate(
            [got[0:1, i * T:(i + 1) * T] for i in range(8)], axis=0
        )
        return carry

    lax.fori_loop(0, SLOTS // 8, row_sums, 0)
    onehot = (slot_row == row_ids[...]).astype(BF16)
    got = jnp.dot(onehot, sums[...].astype(BF16), preferred_element_type=F32)
    for c in range(4):
        row_count[c] = got[c * 8:c * 8 + 8]
    rx = [send(row_count.at[x_at[k]], rx_in.at[k], x_to[k]) for k in range(3)]
    forwards = []
    for k in range(far):
        own[k].wait_recv()
        block = feats.at[core, row_from[k]]
        forwards.append(send(block, block, sibling))
    total = pair_count[...]
    for k in range(far):
        far_counts[k].wait_recv()
        total = total + far_count[k]
    col_scale = 1.0 / jnp.sqrt(1.0 + total)
    scale_keep[...] = col_scale
    turned = jnp.transpose(jnp.concatenate([col_scale, jnp.zeros((96, T), F32)], axis=0))
    own[far].wait_recv()
    for copy in forwards:
        copy.wait_recv()
    for t in range(32):
        block = feats[(t // 2) % 2, t // 4, pl.ds((t % 2) * T, T), :].astype(F32)
        scaled[t] = (block * turned[:, t:t + 1]).astype(BF16)

    list_copy.wait()

    def products(at, term, begin, end, acc):
        def group(g, acc):
            terms = [term(g * GROUP + i) for i in range(GROUP)]
            for i in range(GROUP):
                p = g * GROUP + i
                same = lists[at + 2, 2 * p] == lists[at + 2, 2 * jnp.maximum(p - 1, 0)]
                acc = jnp.where(same, acc, 0.0) + terms[i]
                running[p] = acc
            return acc

        return lax.fori_loop(begin // GROUP, end // GROUP, group, acc)

    def tile_sum(at, t):
        last = lists[at + 3, t]
        before = jnp.where(t > 0, lists[at + 3, jnp.maximum(t - 1, 0)], -1)
        return jnp.where(last > before, running[jnp.maximum(last, 0)], 0.0)

    def forward_term(p):
        spots = [(lists[0, 2 * p + i], lists[1, 2 * p + i]) for i in range(2)]
        left = jnp.concatenate([narrow[s] for s, _ in spots], axis=1)
        right = jnp.concatenate([scaled[c] for _, c in spots], axis=0)
        return jnp.dot(left, right, preferred_element_type=F32)

    products(0, forward_term, 0, PAIRS, jnp.zeros((T, T), F32))

    def put_part(t, carry):
        part[t % 2, t // 2] = tile_sum(0, t).astype(BF16)
        return carry

    lax.fori_loop(0, 32, put_part, 0)
    x_sends = []
    for h in range(2):
        got = {}
        for k in NEAR:
            got[k] = send(part.at[h, pl.ds(x_at[k] * 4, 4)], x_in.at[k, h], x_to[k])
        x_sends.append(got)

    total = row_count[x]
    for k in range(3):
        rx[k].wait_recv()
        total = total + rx_in[k]
    rx_sum[...] = total
    rz = [send(rx_sum, rz_in.at[k], z_to[k]) for k in range(3)]

    def x_total(h):
        for k in NEAR:
            x_sends[h][k].wait_recv()
        z_sends = {}
        for e in (2, 1, 3, 0):
            zc = z if e == 0 else z_at[e - 1]
            total = tile_sum(0, (x * 4 + zc) * 2 + h)
            for k in range(3):
                total = total + x_in[k, h, zc].astype(F32)
            if e:
                z_buf[h, e - 1] = total.astype(BF16)
                z_sends[e - 1] = send(z_buf.at[h, e - 1], z_in.at[h, e - 1], z_to[e - 1])
        return total, z_sends

    def activate(h, total, z_sends, scale):
        for k in range(3):
            z_sends[k].wait_recv()
            total = total + z_in[h, k].astype(F32)
        span = pl.ds(h * T, T)
        pre = scale * split_dot(total, weight[...]) + bias[...]
        sig = jax.nn.sigmoid(pre)
        act_out[span, :] = (pre * sig).astype(BF16)
        grad_pre = cot[span, :].astype(F32) * sig * (1.0 + pre * (1.0 - sig))
        sent = (scale * grad_pre).astype(BF16)
        back[h, col] = lax.dot_general(
            weight[...], sent, (((1,), (1,)), ((), ())), preferred_element_type=F32
        ).astype(BF16)
        mine = back.at[h, col]
        hz = [send(mine, mine, z_to[k]) for k in range(3)]
        hx = [send(mine, mine, x_to[k]) for k in NEAR]
        return total, sent, jnp.sum(grad_pre, axis=0, keepdims=True), hz, hx

    def pass_on(h, hz, hx):
        for k in NEAR[::-1]:
            hz[k].wait_recv()
            block = back.at[h, x * 4 + z_from[k]]
            hx.extend(send(block, block, x_to[j]) for j in NEAR)

    agg0, z_sends0 = x_total(0)
    total = rx_sum[...]
    for k in range(3):
        rz[k].wait_recv()
        total = total + rz_in[k]
    row_scale[...] = 1.0 / jnp.sqrt(1.0 + total)
    scales = []
    for h in range(2):
        turned = jnp.transpose(jnp.broadcast_to(row_scale[pl.ds(2 * z + h, 1), :], (T, T)))
        scales.append(jnp.concatenate([turned, turned], axis=1))
    for copy in held_in[3:]:
        copy.wait()
    agg0, sent0, bias0, hz0, hx0 = activate(0, agg0, z_sends0, scales[0])
    agg1, z_sends1 = x_total(1)
    pass_on(0, hz0, hx0)
    agg1, sent1, bias1, hz1, hx1 = activate(1, agg1, z_sends1, scales[1])

    weight_term = split_dot(jnp.transpose(agg0), sent0) + split_dot(jnp.transpose(agg1), sent1)
    bias_term = jnp.broadcast_to(bias0 + bias1, (8, 256))
    for c in range(2):
        for q in range(8):
            at = (q * 2 + c) * 8
            grads[c, q] = weight_term[at:at + 8]
        grads[c, 8] = bias_term
    gsib = send(grads.at[1 - core], gsib_in, sibling)
    pass_on(1, hz1, hx1)
    gsib.wait_recv()
    for q in range(8):
        gq_buf[q, 0] = grads[core, q] + gsib_in[q]
        gq_buf[q, 1] = grads[core, 8] + gsib_in[8]
    gq_in[here] = gq_buf[here]
    gq = []
    for k, (dz, dy) in enumerate(ROW_STEPS):
        there = ((zl + dz) % 2) * 4 + (y + dy) % 4
        gq.append(send(gq_buf.at[there], gq_in.at[here], row_to[k]))
    for copy in hx0 + hx1:
        copy.wait_recv()

    for copy in gq:
        copy.wait_recv()
    total = gq_in[0]
    for q in range(1, 8):
        total = total + gq_in[q]
    gx_buf[x] = total
    gx = [send(gx_buf.at[x], gx_buf.at[x], x_to[k]) for k in range(3)]

    def backward_term(p):
        spots = [(lists[8, 2 * p + i], lists[9, 2 * p + i]) for i in range(2)]
        left = jnp.concatenate([back[r % 2, r // 2] for _, r in spots], axis=1)
        right = jnp.concatenate([narrow[s] for s, _ in spots], axis=0)
        return jnp.dot(left, right, preferred_element_type=F32)

    acc = products(8, backward_term, 0, PAIRS // 2, jnp.zeros((T, T), F32))
    for copy in gx:
        copy.wait_recv()
    gz_buf[z] = (gx_buf[0] + gx_buf[1]) + (gx_buf[2] + gx_buf[3])
    gz = [send(gz_buf.at[z], gz_buf.at[z], z_to[k]) for k in range(3)]
    products(8, backward_term, PAIRS // 2, PAIRS, acc)

    near = {}
    for dz in (1, 0):
        half = (zl + dz) % 2

        def put_col(i, carry):
            q = half * 4 + i // 2
            col_part[q, i % 2] = tile_sum(8, q * 4 + (1 - core) * 2 + i % 2).astype(BF16)
            return carry

        lax.fori_loop(0, 8, put_col, 0)
        span = pl.ds(half * 4, 4)
        near[dz] = send(col_part.at[span], sib_in.at[span], sibling)
    far_sends = []

    def pair_up(k, dz, dy):
        q = ((zl + dz) % 2) * 4 + (y + dy) % 4
        for h in range(2):
            both = tile_sum(8, q * 4 + core * 2 + h) + sib_in[q, h].astype(F32)
            pair[k, h] = both.astype(BF16)
        far_sends.append(send(pair.at[k], far_in.at[k], row_to[k]))

    near[1].wait_recv()
    for k, (dz, dy) in enumerate(ROW_STEPS):
        if dz == 1:
            pair_up(k, dz, dy)
    for copy in gz:
        copy.wait_recv()
    total = ((gz_buf[0] + gz_buf[1]) + (gz_buf[2] + gz_buf[3])) * factor
    gall[core, here] = total[0]
    bias_out[...] = total[1, 0:1]
    mine = gall.at[core, here]
    ga = [send(mine, mine, device) for device in row_to]
    near[0].wait_recv()
    for k, (dz, dy) in enumerate(ROW_STEPS):
        if dz == 0:
            pair_up(k, dz, dy)
    blocks = [
        tile_sum(8, here * 4 + core * 2 + h) + sib_in[here, h].astype(F32) for h in range(2)
    ]
    for copy in ga:
        copy.wait_recv()
    gs = send(gall.at[core], gall.at[core], sibling)
    for k in range(far):
        far_sends[k].wait_recv()
        blocks = [blocks[h] + far_in[k, h].astype(F32) for h in range(2)]
    for h in range(2):
        block = blocks[h] * scale_keep[pl.ds(row * 2 + h, 1), :]
        feat_out[pl.ds(h * T, T), :] = jnp.transpose(block).astype(BF16)
    gs.wait_recv()
    for c in range(2):
        for q in range(8):
            weight_out[pl.ds((q * 2 + c) * 8, 8), :] = gall[c, q]
    links.drain()
    assert len(links.started) == COPIES


def emit_kernel(*refs):
    for src, dst in zip(refs[:4], refs[4:]):
        dst[...] = src[...]


def on_device(features, weight, bias, cotangent, tile_rows, tile_cols, tile_mask):
    nodes = features.shape[0] * lax.axis_size("row") * lax.axis_size("col")
    vmem = pl.BlockSpec(memory_space=pltpu.VMEM)
    dma = pltpu.SemaphoreType.DMA
    shape = jax.ShapeDtypeStruct
    far = len(ROW_STEPS)
    outs = (
        shape((256, 256), BF16),
        shape((256, T), BF16),
        shape((T, 256), F32),
        shape((1, 256), F32),
    )
    results = pl.pallas_call(
        functools.partial(layer_kernel, 1.0 / float(nodes) ** 0.5),
        out_shape=outs,
        in_specs=[pl.BlockSpec(memory_space=pltpu.HBM)] * 7,
        out_specs=(vmem,) * 4,
        scratch_shapes=[
            pltpu.VMEM((T, 256), BF16),
            pltpu.VMEM((1, 256), F32),
            pltpu.VMEM((256, 256), BF16),
            pltpu.VMEM((1, SLOTS), jnp.int32),
            pltpu.VMEM((1, SLOTS), jnp.int32),
            pltpu.VMEM((SLOTS, T, T), jnp.int32),
            pltpu.VMEM((SLOTS + 1, T, T), BF16),
            pltpu.VMEM((PAIRS, T, T), F32),
            pltpu.VMEM((16, 256), jnp.int32),
            pltpu.VMEM((16, 256), jnp.int32),
            pltpu.SMEM((16, 256), jnp.int32),
            pltpu.VMEM((2, 8, 256, T), BF16),
            pltpu.VMEM((SLOTS, T), F32),
            pltpu.VMEM((32, T), F32),
            pltpu.VMEM((32, T), F32),
            pltpu.VMEM((32, T), F32),
            pltpu.VMEM((far, 32, T), F32),
            pltpu.VMEM((4, 8, T), F32),
            pltpu.VMEM((3, 8, T), F32),
            pltpu.VMEM((8, T), F32),
            pltpu.VMEM((3, 8, T), F32),
            pltpu.VMEM((32, T, T), BF16),
            pltpu.VMEM((2, 16, T, T), BF16),
            pltpu.VMEM((3, 2, 4, T, T), BF16),
            pltpu.VMEM((2, 3, T, T), BF16),
            pltpu.VMEM((2, 3, T, T), BF16),
            pltpu.VMEM((2, 16, T, T), BF16),
            pltpu.VMEM((32, T), F32),
            pltpu.VMEM((8, T), F32),
            pltpu.VMEM((2, 9, 8, 256), F32),
            pltpu.VMEM((9, 8, 256), F32),
            pltpu.VMEM((8, 2, 8, 256), F32),
            pltpu.VMEM((8, 2, 8, 256), F32),
            pltpu.VMEM((4, 2, 8, 256), F32),
            pltpu.VMEM((4, 2, 8, 256), F32),
            pltpu.VMEM((2, 8, 8, 256), F32),
            pltpu.VMEM((8, 2, T, T), BF16),
            pltpu.VMEM((8, 2, T, T), BF16),
            pltpu.VMEM((far, 2, T, T), BF16),
            pltpu.VMEM((far, 2, T, T), BF16),
            dma((SLOTS // CHUNK,)),
            dma,
            dma((6,)),
            dma((COPIES,)),
            dma((COPIES,)),
        ],
        compiler_params=pltpu.CompilerParams(
            vmem_limit_bytes=VMEM_LIMIT, has_side_effects=True, collective_id=1
        ),
        name="layer",
    )(
        features,
        weight,
        bias.reshape(1, 256),
        cotangent,
        tile_rows.reshape(1, SLOTS),
        tile_cols.reshape(1, SLOTS),
        tile_mask.reshape(SLOTS, T, T),
    )
    activations, grad_features, grad_weight, grad_bias = pl.pallas_call(
        emit_kernel,
        out_shape=outs,
        in_specs=[vmem] * 4,
        out_specs=(vmem,) * 4,
        name="emit",
    )(*results)
    return (activations, grad_features, grad_weight, grad_bias.reshape(256))


def solution(mesh):
    placed = (
        P(("col", "row"), None),
        P(),
        P(),
        P(("row", "col"), None),
        P("row", "col", None),
        P("row", "col", None),
        P("row", "col", None, None, None),
    )
    return jax.shard_map(
        on_device,
        mesh=mesh,
        in_specs=placed,
        out_specs=(P(("row", "col"), None), P(("col", "row"), None), P(), P()),
        check_vma=False,
    )
```

time: 712 us -> 77.6 us (0.11)
  waiting for transfers between devices: 321 us -> 0 us
  blocking collectives: 202 us -> 0 us
  matrix products: 87.8 us -> 0 us
  Pallas kernels: 0 us -> 76.9 us
  local copies, waits for them, and re-layouts: 75.1 us -> 0 us
  between operations: 13.9 us -> 0.64 us
  other arithmetic: 10.9 us -> 0 us
    psum x1 -> x0, waiting for transfers between devices: 235 us -> none  [on_device(): lax.psum((weight_term, bias_term), ('row', 'col'))]
    psum x3 -> x0, blocking collectives: 202 us -> none  [the longest x1 76 us: on_device(): lax.psum((weight_term, bias_term), ('row', 'col'))]
    dot_general x9 -> x0, matrix products: 87.8 us -> none  [the longest x1 41.7 us: on_device(): jnp.einsum('sab,sbh->sah', entry_wide, picked, precision=lax.Precision.HI...]
    pallas_call x0 -> x2, Pallas kernels: none -> 76.9 us  [the longest x1 75.2 us: on_device(): pl.pallas_call(functools.partial(layer_kernel, 1.0 / float(nodes) ** 0.5)...]
    all_gather x2 -> x0, waiting for transfers between devices: 58.3 us -> none  [the longest x1 58.2 us: on_device(): gathered = lax.all_gather(sent, 'col', axis=0, tiled=True)]
    dot_general x4 -> x0, local copies, waits for them, and re-layouts: 51.4 us -> none  [the longest x1 21.4 us: on_device(): jnp.einsum('sab,sah->sbh', tile_values, picked_back, preferred_element_ty...]
    reduce_scatter x2 -> x0, waiting for transfers between devices: 27.1 us -> none  [the longest x1 27.1 us: on_device(): lax.psum_scatter(jnp.einsum('st,sah->tah', onehot_rows, products, precisi...]
    gather x2 -> x0, local copies, waits for them, and re-layouts: 22.8 us -> none  [the longest x1 13.3 us: on_device(): picked = scaled.reshape(col_tiles, 128, width)[col_ids]]
  transfers between devices with their start and end apart: 5 -> 0, of which waited for: 3 -> 0; matrix products, arithmetic and copies ran while one was open for 1% -> 0% of each run, Pallas kernels for 0% -> 0%
where the time goes in v2:
time: 77.6 us; the launch traced here: 77.5 us
  Pallas kernels  76.9 us (99%)
    pallas_call x1, Pallas kernels, on_device(): pl.pallas_call(functools.partial(layer_kernel, 1.0 / float(nodes) ** 0.5)...  75.2 us
    pallas_call x1, Pallas kernels, on_device(): pl.pallas_call(emit_kernel, out_shape=outs, in_specs=[vmem] * 4, out_spec...  1.74 us

profile of v2, /device:TPU:1, one launch (start us, length us, event | category | flops | bytes accessed | tf_op | source)
XLA Modules:
  0.0 77.5 jit_solution(18060692898617724475)
XLA Ops:
  0.6 75.2 %layer.1 = (bf16[256,256]{1,0:T(8,128)(2,1)}, bf16[256,128]{1,0:T(8,128)(2,1)}, f32[128,256]{1,0:T(8,128)}, f32[1,256]{1,0:T(1,128)}) custom-call(bf16[256,128]{1,0:T(8,128)(2,1)} %feat.1, bf16[128,256]{1,0:T(8,128)(2,1)} %weight_hbm.1, f32[1,256]{1,0:T(1,128)} %bitcast.6, bf16[256,256]{1,0:T(8,128)(2,1)} %cot_hbm.1, s32[1,160]{1,0:T(1,128)} %bitcast.7, ...), custom_call_target="tpu_custom_call" | custom-call | tf_op jit(solution)/shard_map/layer/pallas_call | solution.py:431
  75.8 1.7 %emit.1 = (bf16[256,256]{1,0:T(8,128)(2,1)}, bf16[256,128]{1,0:T(8,128)(2,1)}, f32[128,256]{1,0:T(8,128)}, f32[1,256]{1,0:T(1,128)}) custom-call(bf16[256,256]{1,0:T(8,128)(2,1)} %get-tuple-element.12.refs_0_, bf16[256,128]{1,0:T(8,128)(2,1)} %get-tuple-element.13.refs_1_, f32[128,256]{1,0:T(8,128)} %get-tuple-element.14.refs_2_, ...), custom_call_target="tpu_custom_call" | custom-call | tf_op jit(solution)/shard_map/emit/pallas_call | solution.py:496

commit v3 on v2

v3 whole, which is shorter than its diff:
```python
import functools

import jax
import jax.numpy as jnp
from jax import lax
from jax.experimental import pallas as pl
from jax.experimental.pallas import tpu as pltpu
from jax.sharding import PartitionSpec as P

F32 = jnp.float32
BF16 = jnp.bfloat16
T = 128
SLOTS = 160
CHUNK = 16
GROUP = 16
PAIRS = (SLOTS + 32) // 2
SENDS = 48
GROUPS = 54
VMEM_LIMIT = 56 * 1024 * 1024
ROW_STEPS = tuple((dz, dy) for dz in (1, 0) for dy in (2, 1, 3, 0) if (dz, dy) != (0, 0))
NEAR = (1, 0, 2)
PIECES = 4
PIECE = 256 // PIECES


class Links:
    def __init__(self, send_sems, recv_sems):
        self.send_sems, self.recv_sems = send_sems, recv_sems
        self.open, self.starts, self.groups = {}, 0, 0

    def group(self):
        self.groups += 1
        return self.groups - 1

    def send(self, src, dst, device, group):
        k = self.starts % SENDS
        self.starts += 1
        if k in self.open:
            self.open[k].wait_send()
        copy = pltpu.make_async_remote_copy(
            src_ref=src,
            dst_ref=dst,
            send_sem=self.send_sems.at[k],
            recv_sem=self.recv_sems.at[group],
            device_id=device,
            device_id_type=pl.DeviceIdType.MESH,
        )
        copy.start()
        self.open[k] = copy

    def wait(self, group, ruler):
        pltpu.make_async_copy(ruler, ruler, self.recv_sems.at[group]).wait()

    def drain(self):
        for copy in self.open.values():
            copy.wait_send()


def split_dot(a, b):
    hi = a.astype(BF16)
    lo = (a - hi.astype(F32)).astype(BF16)
    return jnp.dot(hi, b, preferred_element_type=F32) + jnp.dot(lo, b, preferred_element_type=F32)


def sort_lists(ids, others, lists, at):
    lane = lax.broadcasted_iota(jnp.int32, (1, 256), 1)
    key = (jnp.where(lane < SLOTS, ids, 64) * 256 + lane).astype(F32)
    along = jnp.broadcast_to(key, (256, 256))
    down = jnp.transpose(along)
    wide_lane = lax.broadcasted_iota(jnp.int32, (256, 256), 1).astype(F32)
    id_down = jnp.floor(down * (1.0 / 256.0))
    rank = jnp.sum((along < down).astype(F32), axis=1, keepdims=True)
    held = jnp.sum((id_down == wide_lane).astype(F32), axis=0, keepdims=True)
    odd = held - 2.0 * jnp.floor(held * 0.5)
    below = jnp.sum(jnp.where(wide_lane < id_down, odd, 0.0), axis=1, keepdims=True)
    pos = rank + below
    first = 1.0 - (pos - 2.0 * jnp.floor(pos * 0.5))
    place = jnp.where(id_down < 63.0, (pos == wide_lane).astype(F32), 0.0).astype(BF16)
    row = lax.broadcasted_iota(jnp.int32, (8, 256), 0)
    values = jnp.where(row == 0, lane + 1, jnp.where(row == 1, others, ids))
    moved = jnp.dot(values.astype(F32).astype(BF16), place, preferred_element_type=F32)
    upto = jnp.where(id_down <= wide_lane, first, 0.0)
    last = jnp.sum(upto, axis=0, keepdims=True) - 1.0
    found = jnp.where(row == 3, last, moved).astype(jnp.int32)
    least = jnp.where(row == 3, -1, 0)
    most = jnp.where(row == 0, SLOTS, jnp.where(row == 3, PAIRS - 1, 31))
    lists[pl.ds(at, 8), :] = jnp.minimum(jnp.maximum(found, least), most)


def layer_kernel(
    factor,
    feat, weight_hbm, bias_hbm, cot_hbm, row_hbm, col_hbm, mask,
    act_out, feat_out, weight_out, bias_out,
    weight, bias, cot, row_ids, col_ids,
    mask_in, narrow, running, padded, lists_v, lists,
    feats, sums, count, sib_count, pair_count, pair_send, far_count,
    row_count, rx_in, rx_sum, rz_in, scaled,
    part, x_in, z_buf, z_in, back_in, back,
    scale_keep, row_scale, grads, gsib_in, gq_buf, gq_in, gx_buf, gz_buf, gall,
    col_part, sib_in, pair, far_in,
    mask_sem, list_sem, in_sem, send_sems, recv_sems,
):
    row, col = lax.axis_index("row"), lax.axis_index("col")
    zl, y, core = row // 8, (row // 2) % 4, row % 2
    x, z = col // 4, col % 4
    here = zl * 4 + y
    sibling = (zl * 8 + y * 2 + 1 - core, col)
    row_to = [(((zl + dz) % 2) * 8 + ((y + dy) % 4) * 2 + core, col) for dz, dy in ROW_STEPS]
    row_from = [((zl - dz + 2) % 2) * 4 + (y - dy + 4) % 4 for dz, dy in ROW_STEPS]
    far = len(ROW_STEPS)
    x_at = [(x + d) % 4 for d in (1, 2, 3)]
    z_at = [(z + d) % 4 for d in (1, 2, 3)]
    x_to = [(row, p * 4 + z) for p in x_at]
    z_to = [(row, x * 4 + p) for p in z_at]
    x_from = [(x - d + 4) % 4 for d in (1, 2, 3)]
    z_from = [(z - d + 4) % 4 for d in (1, 2, 3)]
    links = Links(send_sems, recv_sems)
    send, wait, group = links.send, links.wait, links.group

    barrier = pltpu.get_barrier_semaphore()
    peers = [sibling] + row_to + x_to + z_to
    for device in peers:
        pl.semaphore_signal(
            barrier, inc=1, device_id=device, device_id_type=pl.DeviceIdType.MESH
        )
    chunks = SLOTS // CHUNK
    loads = []
    held_in = []
    for k, (src, dst) in enumerate(
        (
            (row_hbm, row_ids),
            (col_hbm, col_ids),
            (feat, feats.at[core, here]),
            (weight_hbm, weight),
            (bias_hbm, bias),
            (cot_hbm, cot),
        )
    ):
        held_in.append(pltpu.make_async_copy(src, dst, in_sem.at[k]))
    for copy in held_in[:2]:
        copy.start()
    for c in range(chunks):
        span = pl.ds(c * CHUNK, CHUNK)
        load = pltpu.make_async_copy(mask.at[span], mask_in.at[span], mask_sem.at[c])
        load.start()
        loads.append(load)
        if c == 1:
            for copy in held_in[2:]:
                copy.start()

    narrow[0] = jnp.zeros((T, T), BF16)

    def take(c):
        loads[c].wait()

        def eight(g, carry):
            at = pl.multiple_of(c * CHUNK + g * 8, 8)
            wide = mask_in[pl.ds(at, 8)].astype(F32)
            narrow[pl.ds(at + 1, 8)] = wide.astype(BF16)
            sums[pl.ds(at, 8), :] = jnp.sum(wide, axis=1)
            return carry

        lax.fori_loop(0, CHUNK // 8, eight, 0)

    for c in range(chunks // 2):
        take(c)
    pl.semaphore_wait(barrier, len(peers))
    held_in[2].wait()
    mine = feats.at[core, here]
    own = [group() for _ in range(far + 1)]
    for k, device in enumerate(row_to + [sibling]):
        send(mine, mine, device, own[k])
    for c in range(chunks // 2, chunks):
        take(c)
    slot_row = lax.broadcasted_iota(jnp.int32, (32, SLOTS), 0)
    for copy in held_in[:2]:
        copy.wait()
    onehot = (slot_row == col_ids[...]).astype(BF16)
    count[...] = jnp.dot(onehot, sums[...].astype(BF16), preferred_element_type=F32)
    near_count = group()
    send(count, sib_count, sibling, near_count)

    wait(near_count, sib_count)
    pair_count[...] = count[...] + sib_count[...]
    pair_send[...] = (pair_count[...].astype(jnp.int32) - SLOTS * T).astype(jnp.int16)
    far_counts = group()
    for k in range(far):
        send(pair_send, far_count.at[k], row_to[k], far_counts)
    padded[...] = jnp.zeros_like(padded)
    padded[0:1, 0:SLOTS] = row_ids[...]
    padded[8:9, 0:SLOTS] = col_ids[...]
    rows_wide, cols_wide = padded[0:1, :], padded[8:9, :]
    sort_lists(rows_wide, cols_wide, lists_v, 0)
    sort_lists(cols_wide, rows_wide, lists_v, 8)
    list_copy = pltpu.make_async_copy(lists_v, lists, list_sem)
    list_copy.start()
    ones = jnp.ones((8, T), BF16)

    def row_sums(g, carry):
        at = pl.multiple_of(g * 8, 8)
        tiles = narrow[pl.ds(at + 1, 8)].reshape(8 * T, T)
        got = lax.dot_general(ones, tiles, (((1,), (1,)), ((), ())), preferred_element_type=F32)
        sums[pl.ds(at, 8), :] = jnp.concatenate(
            [got[0:1, i * T:(i + 1) * T] for i in range(8)], axis=0
        )
        return carry

    lax.fori_loop(0, SLOTS // 8, row_sums, 0)
    onehot = (slot_row == row_ids[...]).astype(BF16)
    got = jnp.dot(onehot, sums[...].astype(BF16), preferred_element_type=F32)
    for c in range(4):
        row_count[c] = got[c * 8:c * 8 + 8]
    rx = group()
    for k in range(3):
        send(row_count.at[x_at[k]], rx_in.at[k], x_to[k], rx)
    forwards = group()
    for k in range(far):
        wait(own[k], feats.at[0, 0])
        block = feats.at[core, row_from[k]]
        send(block, block, sibling, forwards)
    total = pair_count[...]
    wait(far_counts, far_count)
    for k in range(far):
        total = total + (far_count[k].astype(jnp.int32) + SLOTS * T).astype(F32)
    scale_keep[...] = 1.0 / jnp.sqrt(1.0 + total)
    parts = [
        scale_keep[pl.ds((q * 2 + c) * 2, 2), :] for c in (core, 1 - core) for q in range(8)
    ]
    turned = jnp.transpose(jnp.concatenate(parts + [jnp.zeros((96, T), F32)], axis=0))

    def scale_tiles(c, at):
        for q in range(8):
            for h in range(2):
                block = feats[c, q, pl.ds(h * T, T), :].astype(F32)
                lane = at + q * 2 + h
                scaled[(q * 2 + c) * 2 + h] = (block * turned[:, lane:lane + 1]).astype(BF16)

    scale_tiles(core, 0)
    wait(own[far], feats.at[0, 0])
    wait(forwards, feats.at[0, pl.ds(0, far)])
    scale_tiles(1 - core, 16)
    list_copy.wait()

    def half(i):
        return pl.ds(i * 64, 64)

    def products(at, term, rows, begin, end, acc):
        def group_of(g, acc):
            terms = [term(g * GROUP + i, rows) for i in range(GROUP)]
            for i in range(GROUP):
                p = g * GROUP + i
                same = lists[at + 2, 2 * p] == lists[at + 2, 2 * jnp.maximum(p - 1, 0)]
                acc = jnp.where(same, acc, 0.0) + terms[i]
                running[p, rows, :] = acc
            return acc

        return lax.fori_loop(begin // GROUP, end // GROUP, group_of, acc)

    def tile_sum(at, t, rows=pl.ds(0, T)):
        last = lists[at + 3, t]
        before = jnp.where(t > 0, lists[at + 3, jnp.maximum(t - 1, 0)], -1)
        return jnp.where(last > before, running[jnp.maximum(last, 0), rows, :], 0.0)

    def piece_sum(p, chunk):
        return tile_sum(0, chunk * 2 + p // 2, pl.ds(p % 2 * PIECE, PIECE))

    def forward_term(p, rows):
        spots = [(lists[0, 2 * p + i], lists[1, 2 * p + i]) for i in range(2)]
        left = jnp.concatenate([narrow[s, rows, :] for s, _ in spots], axis=1)
        right = jnp.concatenate([scaled[c] for _, c in spots], axis=0)
        return jnp.dot(left, right, preferred_element_type=F32)

    x_sends = [group() for _ in range(PIECES)]
    nothing = jnp.zeros((64, T), F32)
    for i in range(2):

        products(0, forward_term, half(i), 0, PAIRS, nothing)

        for p in (i, i + 2):
            for k in NEAR:
                for zc in range(4):
                    part[p, k, zc] = piece_sum(p, x_at[k] * 4 + zc).astype(BF16)
                send(part.at[p, k], x_in.at[k, p], x_to[k], x_sends[p])

    total = row_count[x]
    wait(rx, rx_in)
    for k in range(3):
        total = total + rx_in[k]
    rx_sum[...] = total
    rz = group()
    for k in range(3):
        send(rx_sum, rz_in.at[k], z_to[k], rz)

    def x_total(p):
        wait(x_sends[p], back.at[0, pl.ds(0, 6)])
        z_sends = group()
        for e in (2, 1, 3, 0):
            zc = z if e == 0 else z_at[e - 1]
            total = piece_sum(p, x * 4 + zc)
            for k in range(3):
                total = total + x_in[k, p, zc].astype(F32)
            if e:
                z_buf[p, e - 1] = total.astype(BF16)
                send(z_buf.at[p, e - 1], z_in.at[p, e - 1], z_to[e - 1], z_sends)
        return total, z_sends

    def activate(p, total, z_sends):
        wait(z_sends, z_in.at[p])
        for k in range(3):
            total = total + z_in[p, k].astype(F32)
        span = pl.ds(p * PIECE, PIECE)
        scale = scales[p // 2][p % 2 * PIECE:p % 2 * PIECE + PIECE]
        pre = scale * split_dot(total, weight[...]) + bias[...]
        sig = jax.nn.sigmoid(pre)
        act_out[span, :] = (pre * sig).astype(BF16)
        grad_pre = cot[span, :].astype(F32) * sig * (1.0 + pre * (1.0 - sig))
        sent = (scale * grad_pre).astype(BF16)
        turned = lax.dot_general(
            weight[...], sent, (((1,), (1,)), ((), ())), preferred_element_type=F32
        )
        back_in[p, col] = jnp.concatenate([turned[:64], turned[64:]], axis=1).astype(BF16)
        mine = back_in.at[p, col]
        for k in (1, 0, 2):
            send(mine, mine, z_to[k], hz[p][k])
        for k in NEAR:
            send(mine, mine, x_to[k], hx[p // 2][3])
        return total, sent, jnp.sum(grad_pre, axis=0, keepdims=True)

    hz = [[group() for _ in range(3)] for _ in range(PIECES)]
    hx = [[group() for _ in range(4)] for _ in range(2)]

    def pass_on(p):
        for k in (0, 2, 1):
            wait(hz[p][k], z_in.at[0, 0])
            block = back_in.at[p, x * 4 + z_from[k]]
            for j in NEAR:
                send(block, block, x_to[j], hx[p // 2][k])

    low = lax.broadcasted_iota(jnp.int32, (64, T), 1) < 64

    def place_back(h):
        for k, zc in ((3, z), (0, z_from[0]), (2, z_from[2]), (1, z_from[1])):
            wait(hx[h][k], back.at[0, pl.ds(0, 3)])
            for xc in range(4):
                j = xc * 4 + zc
                a, b = back_in[2 * h, j].astype(F32), back_in[2 * h + 1, j].astype(F32)
                back[h, j, 0:64] = jnp.where(low, a, pltpu.roll(b, 64, 1)).astype(BF16)
                back[h, j, 64:T] = jnp.where(low, pltpu.roll(a, 64, 1), b).astype(BF16)

    aggs, sents, biases = {}, {}, {}
    sums_x = {}
    sums_x[0] = x_total(0)
    total = rx_sum[...]
    wait(rz, rz_in)
    for k in range(3):
        total = total + rz_in[k]
    row_scale[...] = 1.0 / jnp.sqrt(1.0 + total)
    scales = []
    for h in range(2):
        turned = jnp.transpose(jnp.broadcast_to(row_scale[pl.ds(2 * z + h, 1), :], (T, T)))
        scales.append(jnp.concatenate([turned, turned], axis=1))
    for copy in held_in[3:]:
        copy.wait()

    def act(p):
        aggs[p], sents[p], biases[p] = activate(p, *sums_x[p])

    sums_x[2] = x_total(2)
    act(0)
    sums_x[1] = x_total(1)
    act(2)
    sums_x[3] = x_total(3)
    pass_on(0)
    act(1)
    pass_on(2)
    act(3)
    sent = jnp.concatenate([sents[p] for p in range(PIECES)], axis=0)
    agg = jnp.concatenate([aggs[p] for p in range(PIECES)], axis=0)
    turned = jnp.concatenate([jnp.transpose(agg[:T]), jnp.transpose(agg[T:])], axis=1)
    weight_term = split_dot(turned, sent)
    bias_term = jnp.broadcast_to((biases[0] + biases[1]) + (biases[2] + biases[3]), (8, 256))
    for c in range(2):
        for q in range(8):
            at = (q * 2 + c) * 8
            grads[c, q] = weight_term[at:at + 8]
        grads[c, 8] = bias_term
    gsib = group()
    send(grads.at[1 - core], gsib_in, sibling, gsib)
    pass_on(1)
    wait(gsib, gsib_in)
    for q in range(8):
        gq_buf[q, 0] = grads[core, q] + gsib_in[q]
        gq_buf[q, 1] = grads[core, 8] + gsib_in[8]
    gq_in[here] = gq_buf[here]
    gq = group()
    for k, (dz, dy) in enumerate(ROW_STEPS):
        there = ((zl + dz) % 2) * 4 + (y + dy) % 4
        send(gq_buf.at[there], gq_in.at[here], row_to[k], gq)
    pass_on(3)
    place_back(0)
    wait(gq, gq_in.at[pl.ds(0, far)])
    total = gq_in[0]
    for q in range(1, 8):
        total = total + gq_in[q]
    gz_buf[z] = total
    gz = group()
    for k in range(3):
        send(gz_buf.at[z], gz_buf.at[z], z_to[k], gz)
    place_back(1)

    def backward_term(p, rows):
        spots = [(lists[8, 2 * p + i], lists[9, 2 * p + i]) for i in range(2)]
        left = jnp.concatenate([back[r % 2, r // 2, rows, :] for _, r in spots], axis=1)
        right = jnp.concatenate([narrow[s] for s, _ in spots], axis=0)
        return jnp.dot(left, right, preferred_element_type=F32)

    near = [group(), group()]
    far_sends = [group(), group()]

    def put_col(i):
        for q in range(8):
            for h in range(2):
                t = q * 4 + (1 - core) * 2 + h
                col_part[i, q, h] = tile_sum(8, t, half(i)).astype(BF16)
        send(col_part.at[i], sib_in.at[i], sibling, near[i])

    def pair_up(i):
        wait(near[i], sib_in.at[i])
        for k, (dz, dy) in enumerate(ROW_STEPS):
            q = ((zl + dz) % 2) * 4 + (y + dy) % 4
            for h in range(2):
                own_part = tile_sum(8, q * 4 + core * 2 + h, half(i))
                pair[i, k, h] = (own_part + sib_in[i, q, h].astype(F32)).astype(BF16)
            send(pair.at[i, k], far_in.at[i, k], row_to[k], far_sends[i])

    products(8, backward_term, half(0), 0, PAIRS, nothing)
    put_col(0)
    acc = products(8, backward_term, half(1), 0, PAIRS // 3, nothing)
    pair_up(0)
    wait(gz, gz_buf.at[pl.ds(0, 3)])
    gx_buf[x] = (gz_buf[0] + gz_buf[1]) + (gz_buf[2] + gz_buf[3])
    gx = group()
    for k in range(3):
        send(gx_buf.at[x], gx_buf.at[x], x_to[k], gx)
    products(8, backward_term, half(1), PAIRS // 3, PAIRS, acc)
    put_col(1)
    wait(gx, gx_buf.at[pl.ds(0, 3)])
    total = ((gx_buf[0] + gx_buf[1]) + (gx_buf[2] + gx_buf[3])) * factor
    gall[here, core] = total[0]
    bias_out[...] = total[1, 0:1]
    mine = gall.at[here, core]
    ga = group()
    for device in row_to:
        send(mine, mine, device, ga)
    pair_up(1)
    blocks = [
        jnp.concatenate(
            [
                tile_sum(8, here * 4 + core * 2 + h, half(i)) + sib_in[i, here, h].astype(F32)
                for i in range(2)
            ],
            axis=0,
        )
        for h in range(2)
    ]
    wait(ga, gall.at[pl.ds(0, far), 0])
    held = gall.at[:, core]
    gs = group()
    send(held, held, sibling, gs)
    for i in range(2):
        wait(far_sends[i], far_in.at[i])
    for k in range(far):
        for h in range(2):
            both = jnp.concatenate([far_in[0, k, h], far_in[1, k, h]], axis=0)
            blocks[h] = blocks[h] + both.astype(F32)
    for h in range(2):
        block = blocks[h] * scale_keep[pl.ds(row * 2 + h, 1), :]
        feat_out[pl.ds(h * T, T), :] = jnp.transpose(block).astype(BF16)
    wait(gs, held)
    weight_out[...] = gall[...]
    links.drain()
    assert links.groups <= GROUPS


def emit_kernel(*refs):
    copies = [pltpu.make_async_copy(refs[k], refs[4 + k], refs[8].at[k]) for k in range(4)]
    for copy in copies:
        copy.start()
    for copy in copies:
        copy.wait()


def on_device(features, weight, bias, cotangent, tile_rows, tile_cols, tile_mask):
    nodes = features.shape[0] * lax.axis_size("row") * lax.axis_size("col")
    anywhere = pl.BlockSpec(memory_space=pl.ANY)
    vmem = pl.BlockSpec(memory_space=pltpu.VMEM)
    dma = pltpu.SemaphoreType.DMA
    shape = jax.ShapeDtypeStruct
    far = len(ROW_STEPS)
    outs = (
        shape((256, 256), BF16),
        shape((256, T), BF16),
        shape((8, 2, 8, 256), F32),
        shape((1, 256), F32),
    )
    results = pl.pallas_call(
        functools.partial(layer_kernel, 1.0 / float(nodes) ** 0.5),
        out_shape=tuple(pltpu.VMEM(out.shape, out.dtype) for out in outs),
        in_specs=[pl.BlockSpec(memory_space=pltpu.HBM)] * 7,
        out_specs=(vmem,) * 4,
        scratch_shapes=[
            pltpu.VMEM((T, 256), BF16),
            pltpu.VMEM((1, 256), F32),
            pltpu.VMEM((256, 256), BF16),
            pltpu.VMEM((1, SLOTS), jnp.int32),
            pltpu.VMEM((1, SLOTS), jnp.int32),
            pltpu.VMEM((SLOTS, T, T), jnp.int32),
            pltpu.VMEM((SLOTS + 1, T, T), BF16),
            pltpu.VMEM((PAIRS, T, T), F32),
            pltpu.VMEM((16, 256), jnp.int32),
            pltpu.VMEM((16, 256), jnp.int32),
            pltpu.SMEM((16, 256), jnp.int32),
            pltpu.VMEM((2, 8, 256, T), BF16),
            pltpu.VMEM((SLOTS, T), F32),
            pltpu.VMEM((32, T), F32),
            pltpu.VMEM((32, T), F32),
            pltpu.VMEM((32, T), F32),
            pltpu.VMEM((32, T), jnp.int16),
            pltpu.VMEM((far, 32, T), jnp.int16),
            pltpu.VMEM((4, 8, T), F32),
            pltpu.VMEM((3, 8, T), F32),
            pltpu.VMEM((8, T), F32),
            pltpu.VMEM((3, 8, T), F32),
            pltpu.VMEM((32, T, T), BF16),
            pltpu.VMEM((PIECES, 3, 4, PIECE, T), BF16),
            pltpu.VMEM((3, PIECES, 4, PIECE, T), BF16),
            pltpu.VMEM((PIECES, 3, PIECE, T), BF16),
            pltpu.VMEM((PIECES, 3, PIECE, T), BF16),
            pltpu.VMEM((PIECES, 16, PIECE, T), BF16),
            pltpu.VMEM((2, 16, T, T), BF16),
            pltpu.VMEM((32, T), F32),
            pltpu.VMEM((8, T), F32),
            pltpu.VMEM((2, 9, 8, 256), F32),
            pltpu.VMEM((9, 8, 256), F32),
            pltpu.VMEM((8, 2, 8, 256), F32),
            pltpu.VMEM((8, 2, 8, 256), F32),
            pltpu.VMEM((4, 2, 8, 256), F32),
            pltpu.VMEM((4, 2, 8, 256), F32),
            pltpu.VMEM((8, 2, 8, 256), F32),
            pltpu.VMEM((2, 8, 2, 64, T), BF16),
            pltpu.VMEM((2, 8, 2, 64, T), BF16),
            pltpu.VMEM((2, far, 2, 64, T), BF16),
            pltpu.VMEM((2, far, 2, 64, T), BF16),
            dma((SLOTS // CHUNK,)),
            dma,
            dma((6,)),
            dma((SENDS,)),
            dma((GROUPS,)),
        ],
        compiler_params=pltpu.CompilerParams(
            vmem_limit_bytes=VMEM_LIMIT, has_side_effects=True, collective_id=1
        ),
        name="layer",
    )(
        features,
        weight,
        bias.reshape(1, 256),
        cotangent,
        tile_rows.reshape(1, SLOTS),
        tile_cols.reshape(1, SLOTS),
        tile_mask.reshape(SLOTS, T, T),
    )
    activations, grad_features, grad_weight, grad_bias = pl.pallas_call(
        emit_kernel,
        out_shape=outs,
        in_specs=[vmem] * 4,
        out_specs=(anywhere,) * 4,
        scratch_shapes=[dma((4,))],
        name="emit",
    )(*(pltpu.with_memory_space_constraint(r, pltpu.VMEM) for r in results))
    return (activations, grad_features, grad_weight.reshape(T, 256), grad_bias.reshape(256))


def solution(mesh):
    placed = (
        P(("col", "row"), None),
        P(),
        P(),
        P(("row", "col"), None),
        P("row", "col", None),
        P("row", "col", None),
        P("row", "col", None, None, None),
    )
    return jax.shard_map(
        on_device,
        mesh=mesh,
        in_specs=placed,
        out_specs=(P(("row", "col"), None), P(("col", "row"), None), P(), P()),
        check_vma=False,
    )
```

time: 77.6 us -> 68.9 us (0.89)
  Pallas kernels: 76.9 us -> 68.2 us
    pallas_call x1, Pallas kernels: 75.2 us -> 67.4 us  [on_device(): pl.pallas_call(functools.partial(layer_kernel, 1.0 / float(nodes) ** 0.5)...]
    pallas_call x1, Pallas kernels: 1.74 us -> 0.76 us  [on_device(): pl.pallas_call(emit_kernel, out_shape=outs, in_specs=[vmem] * 4, out_spec...]
where the time goes in v3:
time: 68.9 us; the launch traced here: 68.8 us
  Pallas kernels  68.2 us (99%)
    pallas_call x1, Pallas kernels, on_device(): pl.pallas_call(functools.partial(layer_kernel, 1.0 / float(nodes) ** 0.5)...  67.4 us

profile of v3, /device:TPU:1, one launch (start us, length us, event | category | flops | bytes accessed | tf_op | source)
XLA Modules:
  0.0 68.8 jit_solution(14218133720725462865)
XLA Ops:
  0.6 67.4 %layer.1 = (bf16[256,256]{1,0:T(8,128)(2,1)S(1)}, bf16[256,128]{1,0:T(8,128)(2,1)S(1)}, f32[8,2,8,256]{3,2,1,0:T(8,128)S(1)}, f32[1,256]{1,0:T(1,128)S(1)}) custom-call(bf16[256,128]{1,0:T(8,128)(2,1)} %feat.1, bf16[128,256]{1,0:T(8,128)(2,1)} %weight_hbm.1, f32[1,256]{1,0:T(1,128)} %bitcast.7, bf16[256,256]{1,0:T(8,128)(2,1)} %cot_hbm.1, s32[1,160]{1,0:T(1,128)} %bitcast.8, ...), custom_call_target="tpu_custom_call" | custom-call | tf_op jit(solution)/shard_map/layer/pallas_call | solution.py:506
  68.1 0.8 %emit.1 = (bf16[256,256]{1,0:T(8,128)(2,1)}, bf16[256,128]{1,0:T(8,128)(2,1)}, f32[8,2,8,256]{3,2,1,0:T(8,128)}, f32[1,256]{1,0:T(1,128)}) custom-call(bf16[256,256]{1,0:T(8,128)(2,1)S(1)} %get-tuple-element.12.refs_0_, bf16[256,128]{1,0:T(8,128)(2,1)S(1)} %get-tuple-element.13.refs_1_, f32[8,2,8,256]{3,2,1,0:T(8,128)S(1)} %get-tuple-element.14.refs_2_, ...), custom_call_target="tpu_custom_call" | custom-call | tf_op jit(solution)/shard_map/emit/pallas_call | solution.py:573

commit v4 on v3

--- a/solution.py
+++ b/solution.py
@@ -12,13 +12,13 @@
 T = 128
 SLOTS = 160
 CHUNK = 16
-GROUP = 16
+GROUP = 32
 PAIRS = (SLOTS + 32) // 2
-SENDS = 48
+SENDS = 32
 GROUPS = 54
 VMEM_LIMIT = 56 * 1024 * 1024
 ROW_STEPS = tuple((dz, dy) for dz in (1, 0) for dy in (2, 1, 3, 0) if (dz, dy) != (0, 0))
-NEAR = (1, 0, 2)
+NEAR = (0, 2, 1)
 PIECES = 4
 PIECE = 256 // PIECES
 
@@ -168,8 +168,8 @@
     held_in[2].wait()
     mine = feats.at[core, here]
     own = [group() for _ in range(far + 1)]
-    for k, device in enumerate(row_to + [sibling]):
-        send(mine, mine, device, own[k])
+    for k in (0, 1, 2, 3, 4, far):
+        send(mine, mine, (row_to + [sibling])[k], own[k])
     for c in range(chunks // 2, chunks):
         take(c)
     slot_row = lax.broadcasted_iota(jnp.int32, (32, SLOTS), 0)
@@ -186,6 +186,8 @@
     far_counts = group()
     for k in range(far):
         send(pair_send, far_count.at[k], row_to[k], far_counts)
+    for k in (5, 6):
+        send(mine, mine, row_to[k], own[k])
     padded[...] = jnp.zeros_like(padded)
     padded[0:1, 0:SLOTS] = row_ids[...]
     padded[8:9, 0:SLOTS] = col_ids[...]
@@ -292,7 +294,7 @@
         send(rx_sum, rz_in.at[k], z_to[k], rz)
 
     def x_total(p):
-        wait(x_sends[p], back.at[0, pl.ds(0, 6)])
+        wait(x_sends[p], back.at[pl.ds(0, 6)])
         z_sends = group()
         for e in (2, 1, 3, 0):
             zc = z if e == 0 else z_at[e - 1]
@@ -340,12 +342,12 @@
 
     def place_back(h):
         for k, zc in ((3, z), (0, z_from[0]), (2, z_from[2]), (1, z_from[1])):
-            wait(hx[h][k], back.at[0, pl.ds(0, 3)])
+            wait(hx[h][k], back.at[pl.ds(0, 3)])
             for xc in range(4):
                 j = xc * 4 + zc
                 a, b = back_in[2 * h, j].astype(F32), back_in[2 * h + 1, j].astype(F32)
-                back[h, j, 0:64] = jnp.where(low, a, pltpu.roll(b, 64, 1)).astype(BF16)
-                back[h, j, 64:T] = jnp.where(low, pltpu.roll(a, 64, 1), b).astype(BF16)
+                back[j * 2 + h, 0:64] = jnp.where(low, a, pltpu.roll(b, 64, 1)).astype(BF16)
+                back[j * 2 + h, 64:T] = jnp.where(low, pltpu.roll(a, 64, 1), b).astype(BF16)
 
     aggs, sents, biases = {}, {}, {}
     sums_x = {}
@@ -397,7 +399,6 @@
         there = ((zl + dz) % 2) * 4 + (y + dy) % 4
         send(gq_buf.at[there], gq_in.at[here], row_to[k], gq)
     pass_on(3)
-    place_back(0)
     wait(gq, gq_in.at[pl.ds(0, far)])
     total = gq_in[0]
     for q in range(1, 8):
@@ -406,11 +407,12 @@
     gz = group()
     for k in range(3):
         send(gz_buf.at[z], gz_buf.at[z], z_to[k], gz)
+    place_back(0)
     place_back(1)
 
     def backward_term(p, rows):
         spots = [(lists[8, 2 * p + i], lists[9, 2 * p + i]) for i in range(2)]
-        left = jnp.concatenate([back[r % 2, r // 2, rows, :] for _, r in spots], axis=1)
+        left = jnp.concatenate([back[r, rows, :] for _, r in spots], axis=1)
         right = jnp.concatenate([narrow[s] for s, _ in spots], axis=0)
         return jnp.dot(left, right, preferred_element_type=F32)
 
@@ -436,12 +438,12 @@
     products(8, backward_term, half(0), 0, PAIRS, nothing)
     put_col(0)
     acc = products(8, backward_term, half(1), 0, PAIRS // 3, nothing)
-    pair_up(0)
     wait(gz, gz_buf.at[pl.ds(0, 3)])
     gx_buf[x] = (gz_buf[0] + gz_buf[1]) + (gz_buf[2] + gz_buf[3])
     gx = group()
     for k in range(3):
         send(gx_buf.at[x], gx_buf.at[x], x_to[k], gx)
+    pair_up(0)
     products(8, backward_term, half(1), PAIRS // 3, PAIRS, acc)
     put_col(1)
     wait(gx, gx_buf.at[pl.ds(0, 3)])
@@ -537,7 +539,7 @@
             pltpu.VMEM((PIECES, 3, PIECE, T), BF16),
             pltpu.VMEM((PIECES, 3, PIECE, T), BF16),
             pltpu.VMEM((PIECES, 16, PIECE, T), BF16),
-            pltpu.VMEM((2, 16, T, T), BF16),
+            pltpu.VMEM((32, T, T), BF16),
             pltpu.VMEM((32, T), F32),
             pltpu.VMEM((8, T), F32),
             pltpu.VMEM((2, 9, 8, 256), F32),

time: 68.9 us -> 65.7 us (0.954)
  Pallas kernels: 68.2 us -> 65 us
    pallas_call x1, Pallas kernels: 67.4 us -> 64.2 us  [on_device(): pl.pallas_call(functools.partial(layer_kernel, 1.0 / float(nodes) ** 0.5)...]
where the time goes in v4:
time: 65.7 us; the launch traced here: 65.6 us
  Pallas kernels  65 us (99%)
    pallas_call x1, Pallas kernels, on_device(): pl.pallas_call(functools.partial(layer_kernel, 1.0 / float(nodes) ** 0.5)...  64.2 us

profile of v4, /device:TPU:1, one launch (start us, length us, event | category | flops | bytes accessed | tf_op | source)
XLA Modules:
  0.0 65.6 jit_solution(14922169520653908121)
XLA Ops:
  0.6 64.2 %layer.1 = (bf16[256,256]{1,0:T(8,128)(2,1)S(1)}, bf16[256,128]{1,0:T(8,128)(2,1)S(1)}, f32[8,2,8,256]{3,2,1,0:T(8,128)S(1)}, f32[1,256]{1,0:T(1,128)S(1)}) custom-call(bf16[256,128]{1,0:T(8,128)(2,1)} %feat.1, bf16[128,256]{1,0:T(8,128)(2,1)} %weight_hbm.1, f32[1,256]{1,0:T(1,128)} %bitcast.7, bf16[256,256]{1,0:T(8,128)(2,1)} %cot_hbm.1, s32[1,160]{1,0:T(1,128)} %bitcast.8, ...), custom_call_target="tpu_custom_call" | custom-call | tf_op jit(solution)/shard_map/layer/pallas_call | solution.py:508
  64.9 0.8 %emit.1 = (bf16[256,256]{1,0:T(8,128)(2,1)}, bf16[256,128]{1,0:T(8,128)(2,1)}, f32[8,2,8,256]{3,2,1,0:T(8,128)}, f32[1,256]{1,0:T(1,128)}) custom-call(bf16[256,256]{1,0:T(8,128)(2,1)S(1)} %get-tuple-element.12.refs_0_, bf16[256,128]{1,0:T(8,128)(2,1)S(1)} %get-tuple-element.13.refs_1_, f32[8,2,8,256]{3,2,1,0:T(8,128)S(1)} %get-tuple-element.14.refs_2_, ...), custom_call_target="tpu_custom_call" | custom-call | tf_op jit(solution)/shard_map/emit/pallas_call | solution.py:575

commit v5 on v4

--- a/solution.py
+++ b/solution.py
@@ -11,11 +11,11 @@
 BF16 = jnp.bfloat16
 T = 128
 SLOTS = 160
-CHUNK = 16
+CHUNK = 32
 GROUP = 32
 PAIRS = (SLOTS + 32) // 2
-SENDS = 32
-GROUPS = 54
+SENDS = 24
+GROUPS = 55
 VMEM_LIMIT = 56 * 1024 * 1024
 ROW_STEPS = tuple((dz, dy) for dz in (1, 0) for dy in (2, 1, 3, 0) if (dz, dy) != (0, 0))
 NEAR = (0, 2, 1)
@@ -162,7 +162,7 @@
 
         lax.fori_loop(0, CHUNK // 8, eight, 0)
 
-    for c in range(chunks // 2):
+    for c in range(chunks // 2 + 1):
         take(c)
     pl.semaphore_wait(barrier, len(peers))
     held_in[2].wait()
@@ -170,7 +170,7 @@
     own = [group() for _ in range(far + 1)]
     for k in (0, 1, 2, 3, 4, far):
         send(mine, mine, (row_to + [sibling])[k], own[k])
-    for c in range(chunks // 2, chunks):
+    for c in range(chunks // 2 + 1, chunks):
         take(c)
     slot_row = lax.broadcasted_iota(jnp.int32, (32, SLOTS), 0)
     for copy in held_in[:2]:
@@ -215,32 +215,45 @@
     rx = group()
     for k in range(3):
         send(row_count.at[x_at[k]], rx_in.at[k], x_to[k], rx)
-    forwards = group()
-    for k in range(far):
+    forwards = [group(), group()]
+
+    def forward_block(k):
         wait(own[k], feats.at[0, 0])
         block = feats.at[core, row_from[k]]
-        send(block, block, sibling, forwards)
+        send(block, block, sibling, forwards[k // 5])
+
+    for k in range(5):
+        forward_block(k)
     total = pair_count[...]
     wait(far_counts, far_count)
     for k in range(far):
         total = total + (far_count[k].astype(jnp.int32) + SLOTS * T).astype(F32)
     scale_keep[...] = 1.0 / jnp.sqrt(1.0 + total)
-    parts = [
-        scale_keep[pl.ds((q * 2 + c) * 2, 2), :] for c in (core, 1 - core) for q in range(8)
-    ]
+    order = row_from + [here]
+    parts = [scale_keep[pl.ds((q * 2 + c) * 2, 2), :] for c in (core, 1 - core) for q in order]
     turned = jnp.transpose(jnp.concatenate(parts + [jnp.zeros((96, T), F32)], axis=0))
 
-    def scale_tiles(c, at):
-        for q in range(8):
-            for h in range(2):
-                block = feats[c, q, pl.ds(h * T, T), :].astype(F32)
-                lane = at + q * 2 + h
-                scaled[(q * 2 + c) * 2 + h] = (block * turned[:, lane:lane + 1]).astype(BF16)
-
-    scale_tiles(core, 0)
+    def scale_block(side, k):
+        c, q = (core, 1 - core)[side], order[k]
+        for h in range(2):
+            lane = side * 16 + k * 2 + h
+            block = feats[c, q, pl.ds(h * T, T), :].astype(F32)
+            scaled[(q * 2 + c) * 2 + h] = (block * turned[:, lane:lane + 1]).astype(BF16)
+
+    for k in (far, 0, 1, 2, 3, 4):
+        scale_block(0, k)
+    for k in (5, 6):
+        forward_block(k)
+    scale_block(0, 5)
+    scale_block(0, 6)
     wait(own[far], feats.at[0, 0])
-    wait(forwards, feats.at[0, pl.ds(0, far)])
-    scale_tiles(1 - core, 16)
+    scale_block(1, far)
+    wait(forwards[0], feats.at[0, pl.ds(0, 5)])
+    for k in range(5):
+        scale_block(1, k)
+    wait(forwards[1], feats.at[0, pl.ds(0, 2)])
+    scale_block(1, 5)
+    scale_block(1, 6)
     list_copy.wait()
 
     def half(i):
@@ -443,9 +456,9 @@
     gx = group()
     for k in range(3):
         send(gx_buf.at[x], gx_buf.at[x], x_to[k], gx)
-    pair_up(0)
     products(8, backward_term, half(1), PAIRS // 3, PAIRS, acc)
     put_col(1)
+    pair_up(0)
     wait(gx, gx_buf.at[pl.ds(0, 3)])
     total = ((gx_buf[0] + gx_buf[1]) + (gx_buf[2] + gx_buf[3])) * factor
     gall[here, core] = total[0]

time: 65.7 us -> 65.4 us (level)
  no operation moved by 1% of the time
where the time goes in v5:
time: 65.4 us; the launch traced here: 65.3 us
  Pallas kernels  64.7 us (99%)
    pallas_call x1, Pallas kernels, on_device(): pl.pallas_call(functools.partial(layer_kernel, 1.0 / float(nodes) ** 0.5)...  63.9 us

profile of v5, /device:TPU:1, one launch (start us, length us, event | category | flops | bytes accessed | tf_op | source)
XLA Modules:
  0.0 65.3 jit_solution(6967587163059045617)
XLA Ops:
  0.6 63.9 %layer.1 = (bf16[256,256]{1,0:T(8,128)(2,1)S(1)}, bf16[256,128]{1,0:T(8,128)(2,1)S(1)}, f32[8,2,8,256]{3,2,1,0:T(8,128)S(1)}, f32[1,256]{1,0:T(1,128)S(1)}) custom-call(bf16[256,128]{1,0:T(8,128)(2,1)} %feat.1, bf16[128,256]{1,0:T(8,128)(2,1)} %weight_hbm.1, f32[1,256]{1,0:T(1,128)} %bitcast.7, bf16[256,256]{1,0:T(8,128)(2,1)} %cot_hbm.1, s32[1,160]{1,0:T(1,128)} %bitcast.8, ...), custom_call_target="tpu_custom_call" | custom-call | tf_op jit(solution)/shard_map/layer/pallas_call | solution.py:521
  64.5 0.8 %emit.1 = (bf16[256,256]{1,0:T(8,128)(2,1)}, bf16[256,128]{1,0:T(8,128)(2,1)}, f32[8,2,8,256]{3,2,1,0:T(8,128)}, f32[1,256]{1,0:T(1,128)}) custom-call(bf16[256,256]{1,0:T(8,128)(2,1)S(1)} %get-tuple-element.12.refs_0_, bf16[256,128]{1,0:T(8,128)(2,1)S(1)} %get-tuple-element.13.refs_1_, f32[8,2,8,256]{3,2,1,0:T(8,128)S(1)} %get-tuple-element.14.refs_2_, ...), custom_call_target="tpu_custom_call" | custom-call | tf_op jit(solution)/shard_map/emit/pallas_call | solution.py:588

commit v6 on v5

--- a/solution.py
+++ b/solution.py
@@ -259,17 +259,17 @@
     def half(i):
         return pl.ds(i * 64, 64)
 
-    def products(at, term, rows, begin, end, acc):
+    def products(at, term, rows, begin, end, acc, size=PAIRS // 2):
         def group_of(g, acc):
-            terms = [term(g * GROUP + i, rows) for i in range(GROUP)]
-            for i in range(GROUP):
-                p = g * GROUP + i
+            terms = [term(g * size + i, rows) for i in range(size)]
+            for i in range(size):
+                p = g * size + i
                 same = lists[at + 2, 2 * p] == lists[at + 2, 2 * jnp.maximum(p - 1, 0)]
                 acc = jnp.where(same, acc, 0.0) + terms[i]
                 running[p, rows, :] = acc
             return acc
 
-        return lax.fori_loop(begin // GROUP, end // GROUP, group_of, acc)
+        return lax.fori_loop(begin // size, end // size, group_of, acc)
 
     def tile_sum(at, t, rows=pl.ds(0, T)):
         last = lists[at + 3, t]
@@ -450,13 +450,13 @@
 
     products(8, backward_term, half(0), 0, PAIRS, nothing)
     put_col(0)
-    acc = products(8, backward_term, half(1), 0, PAIRS // 3, nothing)
+    acc = products(8, backward_term, half(1), 0, PAIRS // 3, nothing, GROUP)
     wait(gz, gz_buf.at[pl.ds(0, 3)])
     gx_buf[x] = (gz_buf[0] + gz_buf[1]) + (gz_buf[2] + gz_buf[3])
     gx = group()
     for k in range(3):
         send(gx_buf.at[x], gx_buf.at[x], x_to[k], gx)
-    products(8, backward_term, half(1), PAIRS // 3, PAIRS, acc)
+    products(8, backward_term, half(1), PAIRS // 3, PAIRS, acc, GROUP)
     put_col(1)
     pair_up(0)
     wait(gx, gx_buf.at[pl.ds(0, 3)])

time: 65.4 us -> 65.1 us (level)
  no operation moved by 1% of the time
where the time goes in v6:
time: 65.1 us
  Pallas kernels  64.4 us (99%)
    pallas_call x1, Pallas kernels, on_device(): pl.pallas_call(functools.partial(layer_kernel, 1.0 / float(nodes) ** 0.5)...  63.7 us

profile of v6, /device:TPU:1, one launch (start us, length us, event | category | flops | bytes accessed | tf_op | source)
XLA Modules:
  0.0 65.1 jit_solution(3270700114472146618)
XLA Ops:
  0.6 63.7 %layer.1 = (bf16[256,256]{1,0:T(8,128)(2,1)S(1)}, bf16[256,128]{1,0:T(8,128)(2,1)S(1)}, f32[8,2,8,256]{3,2,1,0:T(8,128)S(1)}, f32[1,256]{1,0:T(1,128)S(1)}) custom-call(bf16[256,128]{1,0:T(8,128)(2,1)} %feat.1, bf16[128,256]{1,0:T(8,128)(2,1)} %weight_hbm.1, f32[1,256]{1,0:T(1,128)} %bitcast.7, bf16[256,256]{1,0:T(8,128)(2,1)} %cot_hbm.1, s32[1,160]{1,0:T(1,128)} %bitcast.8, ...), custom_call_target="tpu_custom_call" | custom-call | tf_op jit(solution)/shard_map/layer/pallas_call | solution.py:521
  64.3 0.8 %emit.1 = (bf16[256,256]{1,0:T(8,128)(2,1)}, bf16[256,128]{1,0:T(8,128)(2,1)}, f32[8,2,8,256]{3,2,1,0:T(8,128)}, f32[1,256]{1,0:T(1,128)}) custom-call(bf16[256,256]{1,0:T(8,128)(2,1)S(1)} %get-tuple-element.12.refs_0_, bf16[256,128]{1,0:T(8,128)(2,1)S(1)} %get-tuple-element.13.refs_1_, f32[8,2,8,256]{3,2,1,0:T(8,128)S(1)} %get-tuple-element.14.refs_2_, ...), custom_call_target="tpu_custom_call" | custom-call | tf_op jit(solution)/shard_map/emit/pallas_call | solution.py:588
